TPU v7x, 128 devices: a whole 4x4x4 slice. The times are simulated.
128 devices in a mesh: box: 8 (over y, core), dir: 16 (over x, z).
Axes of the slice: x: 4, y: 4, z: 4, core: 2. Of those that a mesh axis runs over, the one named last changes fastest.
Arguments:
- leaf_pattern: float32 [2, 6144, 2048], P(None, ('box', 'dir')), may hold values from -6 to 6
- leaf_parent: int32 [128, 48], P(('box', 'dir')), may hold values from 0 to 7, never falling along the last dimension, each value on 1 to 8 neighbouring positions
- octant: int32 [6144], P(('box', 'dir')), may hold values from 0 to 7
- interp_theta: float32 [64, 32], replicated, may hold values from -1 to 1
- interp_phi: float32 [128, 64], replicated, may hold values from -0.75 to 0.75
- shift_angle: float32 [8, 8192], replicated, may hold values from -3.140625 to 3.140625
- near_src: int32 [6144, 16], P(('box', 'dir')), may hold values from 0 to 6143, as said below
- near_type: int32 [6144, 16], P(('box', 'dir')), may hold values from 0 to 315
- leaf_transfer: float32 [2, 316, 2048], replicated, may hold values from -1 to 1
- inter_src: int32 [1024, 32], P('box'), may hold values from 0 to 1023, as said below
- inter_type: int32 [1024, 32], P('box'), may hold values from 0 to 315
- top_transfer: float32 [2, 316, 8192], P(None, None, 'dir'), may hold values from -0.375 to 0.375
Outputs:
- incoming: float32 [2, 1024, 8192], P(None, 'box', 'dir')
- leaf_incoming: float32 [2, 6144, 2048], P(None, ('box', 'dir'))
Inputs may be any that keep to these rules, and one draw needn't show every extreme that they name: `leaf_parent`: along each row the parents never fall, and every parent has 1 to 8 leaves. near_src[i, j] lies within i - 16 to i + 16. inter_src[r, j] lies in box groups r // 128 - 1 to r // 128 + 1, a group being 128 consecutive boxes.
All inputs are finite; a program needn't handle non-finite values.
Results may differ from a plain program's by a relative error of at most 0.0003.
Values sent between devices are 32-bit elements; how exact they have to be, the bound alone decides.
No kernel may reach another device: no remote copies, remote signals or barrier semaphores. Data moves between devices by JAX's collectives and lax.ppermute only.
A program may use at most 192 MiB of HBM per device.

v0:
```python
import jax
import jax.numpy as jnp
from jax import lax
from jax.experimental import pallas as pl
from jax.experimental.pallas import tpu as pltpu
from jax.sharding import PartitionSpec as P

TL = 32
PL = 64
TT = 64
PT = 128
PAR_DEV = 8
REACH = 16
LANES = 128
PAD = 8
F32 = jnp.float32
BF16 = jnp.bfloat16
I32 = jnp.int32
MIB = 1024 * 1024
VMEM = pl.BlockSpec(memory_space=pltpu.VMEM)
SMEM = pl.BlockSpec(memory_space=pltpu.SMEM)
HBM = pl.BlockSpec(memory_space=pltpu.HBM)


def split(x):
    hi = x.astype(BF16)
    lo = (x - hi.astype(F32)).astype(BF16)
    return hi, lo


def cos_sin(x):
    turns = jnp.round(x * 0.63661977236758134)
    r = (x - turns * 1.5703125) - turns * 4.83826794896619e-4
    z = r * r
    s = r + r * z * (-1.6666654611e-1 + z * (8.3321608736e-3 + z * -1.9515295891e-4))
    c = 1.0 - 0.5 * z + z * z * (4.166664568298827e-2 + z * (-1.388731625493765e-3 + z * 2.443315711809948e-5))
    size = jnp.abs(turns)
    odd = size == 1.0
    half = size == 2.0
    big_c = jnp.where(odd, s, c)
    big_s = jnp.where(odd, c, s)
    cosine = jnp.where(half | (turns == 1.0), -big_c, big_c)
    sine = jnp.where(half | (turns == -1.0), -big_s, big_s)
    return cosine, sine


def exchange(x):
    even = lax.broadcasted_iota(I32, x.shape, 0) % 2 == 0
    return jnp.where(even, pltpu.roll(x, x.shape[0] - 1, 0), pltpu.roll(x, 1, 0))


def estimate(microseconds):
    return pl.CostEstimate(flops=1000, bytes_accessed=int(microseconds * 3_000_000), transcendentals=0)


def aggregate_kernel(
    oct_hbm,
    par_hbm,
    x_hbm,
    theta_hbm,
    phi_hbm,
    angle_hbm,
    out_ref,
    low_hbm,
    high_hbm,
    oct_ref,
    par_ref,
    x_ref,
    theta_ref,
    phi_ref,
    angle_ref,
    y_ref,
    ct_ref,
    st_ref,
    sem,
):
    leaves = x_ref.shape[1]
    rows = 2 * TT
    pitch = rows + PAD
    line = TL + PAD
    reach = low_hbm.shape[1]
    gets = [
        pltpu.make_async_copy(source, target, sem.at[i])
        for i, (source, target) in enumerate(
            (
                (angle_hbm, angle_ref),
                (theta_hbm, theta_ref),
                (phi_hbm, phi_ref),
                (x_hbm, x_ref),
                (oct_hbm, oct_ref),
                (par_hbm, par_ref),
            )
        )
    ]
    puts = [
        pltpu.make_async_copy(x_hbm.at[:, 0:reach, :], low_hbm, sem.at[6]),
        pltpu.make_async_copy(x_hbm.at[:, leaves - reach:leaves, :], high_hbm, sem.at[7]),
    ]
    for get in gets:
        get.start()
    for put in puts:
        put.start()
    get_angle, get_theta, get_phi, get_x, get_oct, get_par = gets
    out_ref[...] = jnp.zeros_like(out_ref)
    get_angle.wait()
    for s in range(TT):
        cosine, sine = cos_sin(angle_ref[:, s * LANES:(s + 1) * LANES])
        ct_ref[pl.ds(2 * s, 8, stride=pitch), :] = cosine
        ct_ref[pl.ds(2 * s + 1, 8, stride=pitch), :] = cosine
        st_ref[pl.ds(2 * s, 8, stride=pitch), :] = -sine
        st_ref[pl.ds(2 * s + 1, 8, stride=pitch), :] = sine
    get_theta.wait()
    hi, lo = split(theta_ref[...])
    stack = jnp.concatenate([hi, hi, hi, hi, lo, lo], axis=0)
    row = lax.broadcasted_iota(jnp.int32, (rows, TT), 0)
    col = lax.broadcasted_iota(jnp.int32, (rows, TT), 1)
    pick = jnp.where(row // 2 == col, 1.0, 0.0).astype(BF16)
    dims = (((1,), (1,)), ((), ()))
    wide = lax.dot_general(pick, stack, dims, preferred_element_type=F32)
    row = lax.broadcasted_iota(jnp.int32, wide.shape, 0)
    col = lax.broadcasted_iota(jnp.int32, wide.shape, 1)
    same = row % 2 == (col // TL) % 2
    th = jnp.concatenate([jnp.where(same, wide, 0.0), jnp.where(same, 0.0, wide)], axis=0).astype(BF16)
    get_phi.wait()
    phi = phi_ref[...]
    zero = jnp.zeros_like(phi)
    pair = jnp.concatenate([jnp.concatenate([phi, zero], axis=1), jnp.concatenate([zero, phi], axis=1)], axis=0)
    ph_hi, ph_lo = split(pair)
    ph_two = jnp.concatenate([ph_hi, ph_hi], axis=0)
    get_x.wait()
    for u in range(TL // 2):
        lanes = slice(u * LANES, (u + 1) * LANES)
        block = jnp.concatenate([x_ref[0, :, lanes], x_ref[1, :, lanes]], axis=0)
        hi, lo = split(block)
        y = jnp.dot(jnp.concatenate([hi, lo], axis=1), ph_two, preferred_element_type=F32) + jnp.dot(
            hi, ph_lo, preferred_element_type=F32
        )
        for g in range(0, 2 * leaves, 8):
            y_ref[pl.ds(g * line + 2 * u, 8, stride=line), :] = y[g:g + 8, :LANES]
            y_ref[pl.ds(g * line + 2 * u + 1, 8, stride=line), :] = y[g:g + 8, LANES:]

    def polar(n):
        return jnp.concatenate(
            [
                y_ref[pl.ds(pl.multiple_of(n * line, 8), TL), :],
                y_ref[pl.ds(pl.multiple_of((leaves + n) * line, 8), TL), :],
            ],
            axis=0,
        )

    get_oct.wait()
    get_par.wait()

    def body(m, carry):
        y = jnp.concatenate([polar(2 * m), polar(2 * m + 1)], axis=1)
        hi, lo = split(y)
        f = jnp.dot(th, jnp.concatenate([hi, lo, hi], axis=0), preferred_element_type=F32)
        for k in range(2):
            n = 2 * m + k
            tab = pl.multiple_of(oct_ref[n] * pitch, 8)
            par = pl.multiple_of(par_ref[0, n] * 8, 8)
            lanes = slice(k * LANES, (k + 1) * LANES)
            values = [
                f[8 * d:8 * d + 8, lanes] * ct_ref[pl.ds(tab + 8 * d, 8), :]
                + f[rows + 8 * d:rows + 8 * d + 8, lanes] * st_ref[pl.ds(tab + 8 * d, 8), :]
                for d in range(rows // 8)
            ]
            values = [value + out_ref[d, pl.ds(par, 8), :] for d, value in enumerate(values)]
            for d, value in enumerate(values):
                out_ref[d, pl.ds(par, 8), :] = value
        return carry

    lax.fori_loop(0, leaves // 2, body, 0, unroll=8)
    for put in puts:
        put.wait()


def aggregate(pattern, octs, parents, theta, phi, angle, dirs):
    leaves = pattern.shape[1]
    edge = jax.ShapeDtypeStruct((2, REACH, pattern.shape[2]), F32)
    return pl.pallas_call(
        aggregate_kernel,
        out_shape=(jax.ShapeDtypeStruct((dirs, PAR_DEV * 8, LANES), F32), edge, edge),
        in_specs=[HBM] * 6,
        out_specs=(VMEM, HBM, HBM),
        scratch_shapes=[
            pltpu.SMEM(octs.shape, I32),
            pltpu.SMEM(parents.shape, I32),
            pltpu.VMEM(pattern.shape, F32),
            pltpu.VMEM(theta.shape, F32),
            pltpu.VMEM(phi.shape, F32),
            pltpu.VMEM(angle.shape, F32),
            pltpu.VMEM(((TL + PAD) * 2 * leaves, LANES), F32),
            pltpu.VMEM((8 * (2 * TT + PAD), LANES), F32),
            pltpu.VMEM((8 * (2 * TT + PAD), LANES), F32),
            pltpu.SemaphoreType.DMA((8,)),
        ],
        compiler_params=pltpu.CompilerParams(vmem_limit_bytes=60 * MIB),
        cost_estimate=estimate(5),
        name="aggregate",
    )(octs, parents, pattern, theta, phi, angle)


def prepare_kernel(table_ref, after_hbm, out_ref):
    for t in range(table_ref.shape[0] // 8):
        tile = table_ref[8 * t:8 * t + 8, :]
        out_ref[16 * t:16 * t + 8, :] = tile
        out_ref[16 * t + 8:16 * t + 16, :] = exchange(tile)


def prepare(table, after):
    return pl.pallas_call(
        prepare_kernel,
        out_shape=jax.ShapeDtypeStruct((2 * table.shape[0], LANES), F32),
        in_specs=[VMEM, HBM],
        out_specs=VMEM,
        compiler_params=pltpu.CompilerParams(vmem_limit_bytes=12 * MIB),
        cost_estimate=estimate(1.5),
        name="prepare",
    )(table, after)


def top_kernel(src_ref, type_ref, own_ref, mate_ref, cross_ref, tab_ref, out_ref, box_ref, one_ref, two_ref):
    boxes = own_ref.shape[0] // 8
    entries = src_ref.shape[0] // boxes
    span = 8 * boxes
    box_ref[0:span, :] = own_ref[...]
    box_ref[span:2 * span, :] = mate_ref[...]
    box_ref[2 * span:3 * span, :] = cross_ref[...]

    def body(r, carry):
        one = [jnp.zeros((8, LANES), F32)] * 2
        two = [jnp.zeros((8, LANES), F32)] * 2
        for j in range(entries):
            s = pl.multiple_of(src_ref[j * boxes + r], 8)
            t = pl.multiple_of(type_ref[j * boxes + r], 16)
            a = box_ref[pl.ds(s, 8), :]
            one[j % 2] = one[j % 2] + a * tab_ref[pl.ds(t, 8), :]
            two[j % 2] = two[j % 2] + a * tab_ref[pl.ds(t + 8, 8), :]
        at = pl.ds(pl.multiple_of(8 * r, 8), 8)
        one_ref[at, :] = one[0] + one[1]
        two_ref[at, :] = two[0] + two[1]
        return carry

    lax.fori_loop(0, boxes, body, 0)
    for r in range(0, boxes, 8):
        for c in range(4):
            lanes = slice(c * LANES, (c + 1) * LANES)
            even = pl.ds(8 * r + 2 * c, 8, stride=8)
            odd = pl.ds(8 * r + 2 * c + 1, 8, stride=8)
            out_ref[0, r:r + 8, lanes] = one_ref[even, :] - one_ref[odd, :]
            out_ref[1, r:r + 8, lanes] = two_ref[even, :] + two_ref[odd, :]


def top_translate(src, kind, own, mate, cross, table):
    rows = own.shape[0]
    return pl.pallas_call(
        top_kernel,
        out_shape=jax.ShapeDtypeStruct((2, rows // 8, 4 * LANES), F32),
        in_specs=[SMEM, SMEM, VMEM, VMEM, VMEM, VMEM],
        out_specs=VMEM,
        scratch_shapes=[
            pltpu.VMEM((3 * rows, LANES), F32),
            pltpu.VMEM((rows, LANES), F32),
            pltpu.VMEM((rows, LANES), F32),
        ],
        compiler_params=pltpu.CompilerParams(vmem_limit_bytes=12 * MIB),
        cost_estimate=estimate(9),
        name="top_translate",
    )(src, kind, own, mate, cross, table)


def leaf_kernel(src_ref, type_ref, own_hbm, low_hbm, high_hbm, table_hbm, after_hbm, out_ref, own_ref, low_ref, high_ref, tab_ref, leaf_ref, one_ref, two_ref, sem):
    leaves = own_ref.shape[1]
    reach = low_ref.shape[1]
    chunks = own_ref.shape[2] // LANES
    size = 2 * chunks
    pitch = 2 * size + PAD
    gets = [
        pltpu.make_async_copy(source, target, sem.at[i])
        for i, (source, target) in enumerate(
            ((own_hbm, own_ref), (low_hbm, low_ref), (high_hbm, high_ref), (table_hbm, tab_ref))
        )
    ]
    for get in gets:
        get.start()
    for get in gets[:3]:
        get.wait()
    for ref, start in ((low_ref, 0), (own_ref, reach), (high_ref, reach + leaves)):
        for first in range(0, ref.shape[1], 8):
            for c in range(chunks):
                lanes = slice(c * LANES, (c + 1) * LANES)
                real = ref[0, first:first + 8, lanes]
                imag = ref[1, first:first + 8, lanes]
                at = (start + first) * pitch + 2 * c
                leaf_ref[pl.ds(at, 8, stride=pitch), :] = real
                leaf_ref[pl.ds(at + 1, 8, stride=pitch), :] = imag
                leaf_ref[pl.ds(at + size, 8, stride=pitch), :] = imag
                leaf_ref[pl.ds(at + size + 1, 8, stride=pitch), :] = real
    gets[3].wait()
    line = size + PAD

    def body(i, carry):
        one = jnp.zeros((size, LANES), F32)
        two = jnp.zeros((size, LANES), F32)
        for j in range(src_ref.shape[0]):
            s = pl.multiple_of(src_ref[j, i], 8)
            t = pl.multiple_of(type_ref[j, i], size)
            tab = tab_ref[pl.ds(t, size), :]
            one = one + tab * leaf_ref[pl.ds(s, size), :]
            two = two + tab * leaf_ref[pl.ds(s + size, size), :]
        at = pl.ds(pl.multiple_of(i * line, 8), size)
        one_ref[at, :] = one
        two_ref[at, :] = two
        return carry

    lax.fori_loop(0, leaves, body, 0)
    for first in range(0, leaves, 8):
        for c in range(chunks):
            lanes = slice(c * LANES, (c + 1) * LANES)
            even = pl.ds(first * line + 2 * c, 8, stride=line)
            odd = pl.ds(first * line + 2 * c + 1, 8, stride=line)
            out_ref[0, first:first + 8, lanes] = one_ref[even, :] - one_ref[odd, :]
            out_ref[1, first:first + 8, lanes] = two_ref[even, :] + two_ref[odd, :]


def leaf_translate(src, kind, own, low, high, table, after):
    leaves = own.shape[1]
    reach = low.shape[1]
    size = 2 * own.shape[2] // LANES
    line = size + PAD
    return pl.pallas_call(
        leaf_kernel,
        out_shape=jax.ShapeDtypeStruct(own.shape, F32),
        in_specs=[SMEM, SMEM, HBM, HBM, HBM, HBM, HBM],
        out_specs=VMEM,
        scratch_shapes=[
            pltpu.VMEM(own.shape, F32),
            pltpu.VMEM(low.shape, F32),
            pltpu.VMEM(high.shape, F32),
            pltpu.VMEM(table.shape, F32),
            pltpu.VMEM(((leaves + 2 * reach) * (2 * size + PAD), LANES), F32),
            pltpu.VMEM((leaves * line, LANES), F32),
            pltpu.VMEM((leaves * line, LANES), F32),
            pltpu.SemaphoreType.DMA((4,)),
        ],
        compiler_params=pltpu.CompilerParams(vmem_limit_bytes=40 * MIB),
        cost_estimate=estimate(5),
        name="leaf_translate",
    )(src, kind, own, low, high, table, after)


def interleaved(table):
    types = table.shape[1]
    view = table.reshape(2, types, -1, LANES)
    return view.transpose(1, 2, 0, 3).reshape(-1, LANES)


def per_device(
    leaf_pattern,
    leaf_parent,
    octant,
    interp_theta,
    interp_phi,
    shift_angle,
    near_src,
    near_type,
    leaf_transfer,
    inter_src,
    inter_type,
    top_transfer,
):
    leaves = leaf_pattern.shape[1]
    dirs = lax.axis_size("dir")
    groups = lax.axis_size("box")
    box = lax.axis_index("box")
    parents, low, high = aggregate(
        leaf_pattern, octant, leaf_parent, interp_theta.T, interp_phi.T, shift_angle, dirs
    )
    directed = lax.all_to_all(parents, "dir", split_axis=0, concat_axis=0)
    count = dirs * groups
    leaf_low = lax.ppermute(high, ("box", "dir"), [(i, i + 1) for i in range(count - 1)])
    leaf_high = lax.ppermute(low, ("box", "dir"), [(i + 1, i) for i in range(count - 1)])

    own = directed.reshape(-1, LANES)
    boxes = inter_src.shape[0]
    mate = lax.ppermute(own, "box", [(i, i ^ 1) for i in range(groups)])
    cross = lax.ppermute(own, "box", [(i, ((i + 1) ^ 1) - 1) for i in range(1, groups - 1)])
    table = prepare(interleaved(top_transfer), low)
    src = inter_src.T
    group = src // boxes
    place = jnp.where(group == box, 0, jnp.where(group == (box ^ 1), boxes, 2 * boxes)) + src % boxes
    top_src = (place * 8).reshape(-1)
    top_type = (inter_type.T * 16).reshape(-1)
    incoming = top_translate(top_src, top_type, own, mate, cross, table)

    size = 2 * leaf_pattern.shape[2] // LANES
    first_leaf = lax.axis_index(("box", "dir")) * leaves
    leaf_src = (near_src.T - (first_leaf - REACH)) * (2 * size + PAD)
    leaf_incoming = leaf_translate(
        leaf_src, near_type.T * size, leaf_pattern, leaf_low, leaf_high, interleaved(leaf_transfer), directed
    )
    return (incoming, leaf_incoming)


def solution(mesh):
    return jax.shard_map(
        per_device,
        mesh=mesh,
        in_specs=(
            P(None, ("box", "dir"), None),
            P(("box", "dir"), None),
            P(("box", "dir")),
            P(),
            P(),
            P(),
            P(("box", "dir"), None),
            P(("box", "dir"), None),
            P(),
            P("box", None),
            P("box", None),
            P(None, None, "dir"),
        ),
        out_specs=(P(None, "box", "dir"), P(None, ("box", "dir"), None)),
        check_vma=False,
    )
```

profile of v0, /device:TPU:1, one launch (start us, length us, event | category | flops | bytes accessed | tf_op | source)
XLA Modules:
  0.0 66.7 jit_solution(6043125098028925649)
XLA Ops:
  0.6 17.9 %aggregate.1 = (f32[16,64,128]{2,1,0:T(8,128)}, f32[2,16,2048]{2,1,0:T(8,128)}, f32[2,16,2048]{2,1,0:T(8,128)}) custom-call(s32[48]{0:T(128)} %oct_hbm.1, s32[1,48]{1,0:T(1,128)} %par_hbm.1, f32[2,48,2048]{2,1,0:T(8,128)} %own_hbm.1, f32[32,64]{1,0:T(8,128)} %bitcast.47, f32[64,128]{1,0:T(8,128)} %bitcast.46, f32[8,8192]{1,0:T(8,128)} %angle_hbm.1), custom_call_target="tpu_custom_call" | custom-call | flops 1000 | bytes 15000000 | tf_op jit(solution)/shard_map/aggregate/pallas_call | solution.py:181
  18.5 0.0 copy-start.4
  18.5 0.0 copy-start.5
  18.5 8.4 %all-to-all-start = ((f32[16,64,128]{2,1,0:T(8,128)}), f32[16,64,128]{2,1,0:T(8,128)S(1)}, u32[]{:S(2)}, u32[]{:S(2)}) async-start(f32[16,64,128]{2,1,0:T(8,128)} %get-tuple-element.5), calls=%async_computation | async-start | bytes 1048576 | tf_op jit(solution)/shard_map/all_to_all | solution.py:380
  27.0 7.7 %collective-permute-start.3 = (f32[2,16,2048]{2,1,0:T(8,128)}, f32[2,16,2048]{2,1,0:T(8,128)S(1)}, u32[]{:S(2)}, u32[]{:S(2)}) collective-permute-start(f32[2,16,2048]{2,1,0:T(8,128)} %get-tuple-element.6.after_hbm), channel_id=1, source_target_pairs={{1,0},{2,1},{3,2},{4,3},{5,4},{6,5},{7,6},{8,7},{9,8},{10,9},{11,1... | collective-permute-start | bytes 786440 | tf_op jit(solution)/shard_map/ppermute | solution.py:383
  34.7 1.9 %collective-permute-start.2 = (f32[2,16,2048]{2,1,0:T(8,128)}, f32[2,16,2048]{2,1,0:T(8,128)}, u32[]{:S(2)}, u32[]{:S(2)}) collective-permute-start(f32[2,16,2048]{2,1,0:T(8,128)} %get-tuple-element.7), channel_id=1, source_target_pairs={{0,1},{1,2},{2,3},{3,4},{4,5},{5,6},{6,7},{7,8},{8,9},{9,10},{10,1... | collective-permute-start | bytes 786440 | tf_op jit(solution)/shard_map/ppermute | solution.py:382
  36.6 0.7 all-to-all-done.after_hbm
  37.3 2.2 %collective-permute-start = (f32[1024,128]{1,0:T(8,128)S(1)}, f32[1024,128]{1,0:T(8,128)}, u32[]{:S(2)}, u32[]{:S(2)}) collective-permute-start(f32[1024,128]{1,0:T(8,128)S(1)} %bitcast.42), channel_id=1, source_target_pairs={{0,16},{16,0},{32,48},{48,32},{64,80},{80,64},{96,112},{112,96},{1... | collective-permute-start | bytes 1572872 | tf_op jit(solution)/shard_map/ppermute | solution.py:387
  39.5 3.1 %collective-permute-start.1 = (f32[1024,128]{1,0:T(8,128)S(1)}, f32[1024,128]{1,0:T(8,128)}, u32[]{:S(2)}, u32[]{:S(2)}) collective-permute-start(f32[1024,128]{1,0:T(8,128)S(1)} %bitcast.43), channel_id=1, source_target_pairs={{16,32},{32,16},{48,64},{64,48},{80,96},{96,80},{17,33},{33,17},{4... | collective-permute-start | bytes 1572872 | tf_op jit(solution)/shard_map/ppermute | solution.py:388
  42.5 0.7 %multiply_bitcast_fusion.type_ref = s32[4096]{0:T(1024)S(1)} fusion(s32[128,32]{0,1:T(8,128)} %param.22), kind=kLoop, calls=%fused_computation.11 | loop fusion | flops 4096 | bytes 32768 | tf_op jit(solution)/shard_map/reshape | solution.py:394
  43.3 0.7 %fusion.2.src_ref = s32[4096]{0:T(1024)S(1)} fusion(s32[128,32]{0,1:T(8,128)} %param.21, s32[]{:T(128)S(6)} %xor.3, s32[]{:T(128)S(6)} %axis_index.27), kind=kLoop, calls=%fused_computation.7 | loop fusion | flops 102400 | bytes 32776 | tf_op jit(solution)/shard_map/reshape | solution.py:393
  44.0 0.0 copy-start.2
  44.0 1.3 %copy-done.2 = f32[2,316,512]{2,0,1:T(2,128)S(1)} copy-done((f32[2,316,512]{2,0,1:T(2,128)S(1)}, f32[2,316,512]{2,0,1:T(2,128)}, u32[]{:S(2)}) %copy-start.2) | copy-done | bytes 1294360
  45.3 0.0 copy-start.3
  45.3 0.9 %copy-done.3 = f32[2,16,2048]{2,1,0:T(8,128)S(1)} copy-done((f32[2,16,2048]{2,1,0:T(8,128)S(1)}, f32[2,16,2048]{2,1,0:T(8,128)}, u32[]{:S(2)}) %copy-start.3) | copy-done | bytes 262168
  46.3 0.2 prepare.1.tab_ref
  46.5 0.0 copy-done.4
  46.5 0.0 copy-done.5
  46.5 0.0 collective-permute-done.3.high_hbm
  46.5 1.8 %collective-permute-done.2.low_hbm = f32[2,16,2048]{2,1,0:T(8,128)} collective-permute-done((f32[2,16,2048]{2,1,0:T(8,128)}, f32[2,16,2048]{2,1,0:T(8,128)}, u32[]{:S(2)}, u32[]{:S(2)}) %collective-permute-start.2) | collective-permute-done | bytes 262176 | tf_op jit(solution)/shard_map/ppermute | solution.py:382
  48.3 0.0 copy-start
  48.3 2.5 %copy-done = f32[2,316,2048]{2,0,1:T(2,128)S(1)} copy-done((f32[2,316,2048]{2,0,1:T(2,128)S(1)}, f32[2,316,2048]{2,0,1:T(2,128)}, u32[]{:S(2)}) %copy-start) | copy-done | bytes 5177368
  50.8 0.0 copy-start.1
  50.8 1.1 %copy-done.1 = f32[2,48,2048]{2,1,0:T(8,128)S(1)} copy-done((f32[2,48,2048]{2,1,0:T(8,128)S(1)}, f32[2,48,2048]{2,1,0:T(8,128)}, u32[]{:S(2)}) %copy-start.1) | copy-done | bytes 786456
  51.9 6.3 %leaf_translate.1 = f32[2,48,2048]{2,1,0:T(8,128)} custom-call(s32[16,48]{1,0:T(8,128)S(1)} %get-tuple-element.9.src_ref, s32[16,48]{1,0:T(8,128)S(1)} %get-tuple-element.8.type_ref, f32[2,48,2048]{2,1,0:T(8,128)S(1)} %copy-done.1, f32[2,16,2048]{2,1,0:T(8,128)} %collective-permute-done.2.low_hbm, f32[2,16,2048]{2,1,0:T(8,128)S(1)} %collective-permute-done.3.high_hbm, ...), custom_call_target="tpu_custom_call" | custom-call | flops 1000 | bytes 15000000 | tf_op jit(solution)/shard_map/leaf_translate/pallas_call | solution.py:332
  58.2 0.0 collective-permute-done.mate_ref
  58.2 0.0 collective-permute-done.1.cross_ref
  58.2 8.5 %top_translate.1 = f32[2,128,512]{2,1,0:T(8,128)} custom-call(s32[4096]{0:T(1024)S(1)} %fusion.2.src_ref, s32[4096]{0:T(1024)S(1)} %multiply_bitcast_fusion.type_ref, f32[1024,128]{1,0:T(8,128)S(1)} %bitcast.44, f32[1024,128]{1,0:T(8,128)} %collective-permute-done.mate_ref, f32[1024,128]{1,0:T(8,128)} %collective-permute-done.1.cross_ref, ...), custom_call_target="tpu_custom_call" | custom-call | flops 1000 | bytes 27000000 | tf_op jit(solution)/shard_map/top_translate/pallas_call | solution.py:257
  (1 shorter events, 0.0 us)
Async XLA Ops:
  18.5 28.0 %copy-start.4 = (s32[48,16]{0,1:T(8,128)S(1)}, s32[48,16]{0,1:T(8,128)}, u32[]{:S(2)}) copy-start(s32[48,16]{0,1:T(8,128)} %param.19) | copy-start | bytes 9220
  18.5 28.0 %copy-start.5 = (s32[48,16]{0,1:T(8,128)S(1)}, s32[48,16]{0,1:T(8,128)}, u32[]{:S(2)}) copy-start(s32[48,16]{0,1:T(8,128)} %param.18) | copy-start | bytes 9220
  18.5 18.7 %all-to-all-start = ((f32[16,64,128]{2,1,0:T(8,128)}), f32[16,64,128]{2,1,0:T(8,128)S(1)}, u32[]{:S(2)}, u32[]{:S(2)}) async-start(f32[16,64,128]{2,1,0:T(8,128)} %get-tuple-element.5), calls=%async_computation | async-start | bytes 1048576 | tf_op jit(solution)/shard_map/all_to_all | solution.py:380
  27.0 19.5 %collective-permute-start.3 = (f32[2,16,2048]{2,1,0:T(8,128)}, f32[2,16,2048]{2,1,0:T(8,128)S(1)}, u32[]{:S(2)}, u32[]{:S(2)}) collective-permute-start(f32[2,16,2048]{2,1,0:T(8,128)} %get-tuple-element.6.after_hbm), channel_id=1, source_target_pairs={{1,0},{2,1},{3,2},{4,3},{5,4},{6,5},{7,6},{8,7},{9,8},{10,9},{11,1... | collective-permute-start | bytes 786440 | tf_op jit(solution)/shard_map/ppermute | solution.py:383
  34.7 13.6 %collective-permute-start.2 = (f32[2,16,2048]{2,1,0:T(8,128)}, f32[2,16,2048]{2,1,0:T(8,128)}, u32[]{:S(2)}, u32[]{:S(2)}) collective-permute-start(f32[2,16,2048]{2,1,0:T(8,128)} %get-tuple-element.7), channel_id=1, source_target_pairs={{0,1},{1,2},{2,3},{3,4},{4,5},{5,6},{6,7},{7,8},{8,9},{9,10},{10,1... | collective-permute-start | bytes 786440 | tf_op jit(solution)/shard_map/ppermute | solution.py:382
  37.3 21.0 %collective-permute-start = (f32[1024,128]{1,0:T(8,128)S(1)}, f32[1024,128]{1,0:T(8,128)}, u32[]{:S(2)}, u32[]{:S(2)}) collective-permute-start(f32[1024,128]{1,0:T(8,128)S(1)} %bitcast.42), channel_id=1, source_target_pairs={{0,16},{16,0},{32,48},{48,32},{64,80},{80,64},{96,112},{112,96},{1... | collective-permute-start | bytes 1572872 | tf_op jit(solution)/shard_map/ppermute | solution.py:387
  39.5 18.8 %collective-permute-start.1 = (f32[1024,128]{1,0:T(8,128)S(1)}, f32[1024,128]{1,0:T(8,128)}, u32[]{:S(2)}, u32[]{:S(2)}) collective-permute-start(f32[1024,128]{1,0:T(8,128)S(1)} %bitcast.43), channel_id=1, source_target_pairs={{16,32},{32,16},{48,64},{64,48},{80,96},{96,80},{17,33},{33,17},{4... | collective-permute-start | bytes 1572872 | tf_op jit(solution)/shard_map/ppermute | solution.py:388
  44.0 1.3 %copy-start.2 = (f32[2,316,512]{2,0,1:T(2,128)S(1)}, f32[2,316,512]{2,0,1:T(2,128)}, u32[]{:S(2)}) copy-start(f32[2,316,512]{2,0,1:T(2,128)} %param.23) | copy-start | bytes 3883012
  45.3 0.9 %copy-start.3 = (f32[2,16,2048]{2,1,0:T(8,128)S(1)}, f32[2,16,2048]{2,1,0:T(8,128)}, u32[]{:S(2)}) copy-start(f32[2,16,2048]{2,1,0:T(8,128)} %get-tuple-element.6.after_hbm) | copy-start | bytes 786436
  48.3 2.5 %copy-start = (f32[2,316,2048]{2,0,1:T(2,128)S(1)}, f32[2,316,2048]{2,0,1:T(2,128)}, u32[]{:S(2)}) copy-start(f32[2,316,2048]{2,0,1:T(2,128)} %param.20) | copy-start | bytes 15532036
  50.8 1.1 %copy-start.1 = (f32[2,48,2048]{2,1,0:T(8,128)S(1)}, f32[2,48,2048]{2,1,0:T(8,128)}, u32[]{:S(2)}) copy-start(f32[2,48,2048]{2,1,0:T(8,128)} %own_hbm.1) | copy-start | bytes 2359300
where the time goes:
time: 67.3 us; the launch traced here: 66.7 us
  Pallas kernels  32.8 us (49%)
  starting transfers between devices  23.3 us (35%)
  local copies, waits for them, and re-layouts  5.87 us (9%)
  waiting for transfers between devices  2.45 us (4%)
  other arithmetic  1.47 us (2%)
  between operations  0.77 us (1%)
    pallas_call x1, Pallas kernels, aggregate(): pl.pallas_call(aggregate_kernel, out_shape=(jax.ShapeDtypeStruct((dirs, P...  17.9 us
    pallas_call x1, Pallas kernels, top_translate(): pl.pallas_call(top_kernel, out_shape=jax.ShapeDtypeStruct((2, rows // 8,...  8.48 us
    all_to_all x1, starting transfers between devices, per_device(): directed = lax.all_to_all(parents, 'dir', split_axis=0, concat_axis=0)  8.44 us
    ppermute x1, starting transfers between devices, per_device(): lax.ppermute(low, ('box', 'dir'), [(i + 1, i) for i in range(count - 1)])  7.71 us
    pallas_call x1, Pallas kernels, leaf_translate(): pl.pallas_call(leaf_kernel, out_shape=jax.ShapeDtypeStruct(own.shape, F32...  6.3 us
    unnamed x12, local copies, waits for them, and re-layouts  5.87 us
    ppermute x1, starting transfers between devices, per_device(): lax.ppermute(own, 'box', [(i, (i + 1 ^ 1) - 1) for i in range(1, groups -...  3.08 us
    ppermute x1, starting transfers between devices, per_device(): mate = lax.ppermute(own, 'box', [(i, i ^ 1) for i in range(groups)])  2.19 us
  transfers between devices with their start and end apart: 5, of which 2 were waited for; matrix products, arithmetic and copies ran while one was open for 2% of the time, Pallas kernels for 10%

commit v1 on v0

--- a/solution.py
+++ b/solution.py
@@ -61,8 +61,8 @@
     phi_hbm,
     angle_hbm,
     out_ref,
-    low_hbm,
-    high_hbm,
+    edge_b_hbm,
+    edge_a_hbm,
     oct_ref,
     par_ref,
     x_ref,
@@ -78,7 +78,7 @@
     rows = 2 * TT
     pitch = rows + PAD
     line = TL + PAD
-    reach = low_hbm.shape[1]
+    reach = edge_b_hbm.shape[1]
     gets = [
         pltpu.make_async_copy(source, target, sem.at[i])
         for i, (source, target) in enumerate(
@@ -92,14 +92,15 @@
             )
         )
     ]
+    last = leaves - reach
+    start_a = pl.multiple_of(jnp.where(lax.axis_index("dir") % 2 == 0, last, 0), 8)
+    start_b = pl.multiple_of(last - start_a, 8)
     puts = [
-        pltpu.make_async_copy(x_hbm.at[:, 0:reach, :], low_hbm, sem.at[6]),
-        pltpu.make_async_copy(x_hbm.at[:, leaves - reach:leaves, :], high_hbm, sem.at[7]),
+        pltpu.make_async_copy(x_ref.at[:, pl.ds(start_b, reach), :], edge_b_hbm, sem.at[6]),
+        pltpu.make_async_copy(x_ref.at[:, pl.ds(start_a, reach), :], edge_a_hbm, sem.at[7]),
     ]
     for get in gets:
         get.start()
-    for put in puts:
-        put.start()
     get_angle, get_theta, get_phi, get_x, get_oct, get_par = gets
     out_ref[...] = jnp.zeros_like(out_ref)
     get_angle.wait()
@@ -128,6 +129,8 @@
     ph_hi, ph_lo = split(pair)
     ph_two = jnp.concatenate([ph_hi, ph_hi], axis=0)
     get_x.wait()
+    for put in puts:
+        put.start()
     for u in range(TL // 2):
         lanes = slice(u * LANES, (u + 1) * LANES)
         block = jnp.concatenate([x_ref[0, :, lanes], x_ref[1, :, lanes]], axis=0)
@@ -201,48 +204,51 @@
     )(octs, parents, pattern, theta, phi, angle)
 
 
-def prepare_kernel(table_ref, after_hbm, out_ref):
+def top_kernel(
+    src_ref, type_ref, own_hbm, mate_hbm, cross_hbm, table_hbm, out_ref, box_ref, table_ref, tab_ref, one_ref, two_ref, sem
+):
+    span = own_hbm.shape[0]
+    boxes = span // 8
+    entries = src_ref.shape[0] // boxes
+    gets = [
+        pltpu.make_async_copy(source, target, sem.at[i])
+        for i, (source, target) in enumerate(
+            (
+                (table_hbm, table_ref),
+                (own_hbm, box_ref.at[0:span, :]),
+                (mate_hbm, box_ref.at[span:2 * span, :]),
+                (cross_hbm, box_ref.at[2 * span:3 * span, :]),
+            )
+        )
+    ]
+    for get in gets:
+        get.start()
+    gets[0].wait()
     for t in range(table_ref.shape[0] // 8):
         tile = table_ref[8 * t:8 * t + 8, :]
-        out_ref[16 * t:16 * t + 8, :] = tile
-        out_ref[16 * t + 8:16 * t + 16, :] = exchange(tile)
-
-
-def prepare(table, after):
-    return pl.pallas_call(
-        prepare_kernel,
-        out_shape=jax.ShapeDtypeStruct((2 * table.shape[0], LANES), F32),
-        in_specs=[VMEM, HBM],
-        out_specs=VMEM,
-        compiler_params=pltpu.CompilerParams(vmem_limit_bytes=12 * MIB),
-        cost_estimate=estimate(1.5),
-        name="prepare",
-    )(table, after)
-
-
-def top_kernel(src_ref, type_ref, own_ref, mate_ref, cross_ref, tab_ref, out_ref, box_ref, one_ref, two_ref):
-    boxes = own_ref.shape[0] // 8
-    entries = src_ref.shape[0] // boxes
-    span = 8 * boxes
-    box_ref[0:span, :] = own_ref[...]
-    box_ref[span:2 * span, :] = mate_ref[...]
-    box_ref[2 * span:3 * span, :] = cross_ref[...]
-
-    def body(r, carry):
-        one = [jnp.zeros((8, LANES), F32)] * 2
-        two = [jnp.zeros((8, LANES), F32)] * 2
+        tab_ref[16 * t:16 * t + 8, :] = tile
+        tab_ref[16 * t + 8:16 * t + 16, :] = exchange(tile)
+    for get in gets[1:]:
+        get.wait()
+    together = 8
+
+    def body(m, carry):
+        one = [jnp.zeros((8, LANES), F32) for _ in range(together)]
+        two = [jnp.zeros((8, LANES), F32) for _ in range(together)]
         for j in range(entries):
-            s = pl.multiple_of(src_ref[j * boxes + r], 8)
-            t = pl.multiple_of(type_ref[j * boxes + r], 16)
-            a = box_ref[pl.ds(s, 8), :]
-            one[j % 2] = one[j % 2] + a * tab_ref[pl.ds(t, 8), :]
-            two[j % 2] = two[j % 2] + a * tab_ref[pl.ds(t + 8, 8), :]
-        at = pl.ds(pl.multiple_of(8 * r, 8), 8)
-        one_ref[at, :] = one[0] + one[1]
-        two_ref[at, :] = two[0] + two[1]
+            for k in range(together):
+                s = pl.multiple_of(src_ref[j * boxes + m * together + k], 8)
+                t = pl.multiple_of(type_ref[j * boxes + m * together + k], 16)
+                a = box_ref[pl.ds(s, 8), :]
+                one[k] = one[k] + a * tab_ref[pl.ds(t, 8), :]
+                two[k] = two[k] + a * tab_ref[pl.ds(t + 8, 8), :]
+        for k in range(together):
+            at = pl.ds(pl.multiple_of(8 * (m * together + k), 8), 8)
+            one_ref[at, :] = one[k]
+            two_ref[at, :] = two[k]
         return carry
 
-    lax.fori_loop(0, boxes, body, 0)
+    lax.fori_loop(0, boxes // together, body, 0)
     for r in range(0, boxes, 8):
         for c in range(4):
             lanes = slice(c * LANES, (c + 1) * LANES)
@@ -257,47 +263,78 @@
     return pl.pallas_call(
         top_kernel,
         out_shape=jax.ShapeDtypeStruct((2, rows // 8, 4 * LANES), F32),
-        in_specs=[SMEM, SMEM, VMEM, VMEM, VMEM, VMEM],
+        in_specs=[SMEM, SMEM, HBM, HBM, HBM, HBM],
         out_specs=VMEM,
         scratch_shapes=[
             pltpu.VMEM((3 * rows, LANES), F32),
+            pltpu.VMEM(table.shape, F32),
+            pltpu.VMEM((2 * table.shape[0], LANES), F32),
             pltpu.VMEM((rows, LANES), F32),
             pltpu.VMEM((rows, LANES), F32),
+            pltpu.SemaphoreType.DMA((4,)),
         ],
-        compiler_params=pltpu.CompilerParams(vmem_limit_bytes=12 * MIB),
+        compiler_params=pltpu.CompilerParams(vmem_limit_bytes=24 * MIB),
         cost_estimate=estimate(9),
         name="top_translate",
     )(src, kind, own, mate, cross, table)
 
 
-def leaf_kernel(src_ref, type_ref, own_hbm, low_hbm, high_hbm, table_hbm, after_hbm, out_ref, own_ref, low_ref, high_ref, tab_ref, leaf_ref, one_ref, two_ref, sem):
-    leaves = own_ref.shape[1]
-    reach = low_ref.shape[1]
-    chunks = own_ref.shape[2] // LANES
+def leaf_kernel(
+    src_hbm,
+    type_hbm,
+    own_hbm,
+    pair_a_hbm,
+    pair_b_hbm,
+    table_hbm,
+    after_hbm,
+    out_ref,
+    src_ref,
+    type_ref,
+    near_ref,
+    tab_ref,
+    leaf_ref,
+    one_ref,
+    two_ref,
+    sem,
+):
+    leaves = own_hbm.shape[1]
+    reach = pair_a_hbm.shape[1]
+    chunks = own_hbm.shape[2] // LANES
     size = 2 * chunks
     pitch = 2 * size + PAD
+    odd = lax.axis_index("dir") % 2
+    after = reach + leaves
+    place_a = pl.multiple_of((1 - odd) * after, 8)
+    place_b = pl.multiple_of(odd * after, 8)
     gets = [
         pltpu.make_async_copy(source, target, sem.at[i])
         for i, (source, target) in enumerate(
-            ((own_hbm, own_ref), (low_hbm, low_ref), (high_hbm, high_ref), (table_hbm, tab_ref))
+            (
+                (table_hbm, tab_ref),
+                (own_hbm, near_ref.at[:, reach:after, :]),
+                (pair_a_hbm, near_ref.at[:, pl.ds(place_a, reach), :]),
+                (pair_b_hbm, near_ref.at[:, pl.ds(place_b, reach), :]),
+                (src_hbm, src_ref),
+                (type_hbm, type_ref),
+            )
         )
     ]
     for get in gets:
         get.start()
-    for get in gets[:3]:
+    for get in gets[1:4]:
         get.wait()
-    for ref, start in ((low_ref, 0), (own_ref, reach), (high_ref, reach + leaves)):
-        for first in range(0, ref.shape[1], 8):
-            for c in range(chunks):
-                lanes = slice(c * LANES, (c + 1) * LANES)
-                real = ref[0, first:first + 8, lanes]
-                imag = ref[1, first:first + 8, lanes]
-                at = (start + first) * pitch + 2 * c
-                leaf_ref[pl.ds(at, 8, stride=pitch), :] = real
-                leaf_ref[pl.ds(at + 1, 8, stride=pitch), :] = imag
-                leaf_ref[pl.ds(at + size, 8, stride=pitch), :] = imag
-                leaf_ref[pl.ds(at + size + 1, 8, stride=pitch), :] = real
-    gets[3].wait()
+    for first in range(0, near_ref.shape[1], 8):
+        for c in range(chunks):
+            lanes = slice(c * LANES, (c + 1) * LANES)
+            real = near_ref[0, first:first + 8, lanes]
+            imag = near_ref[1, first:first + 8, lanes]
+            at = first * pitch + 2 * c
+            leaf_ref[pl.ds(at, 8, stride=pitch), :] = real
+            leaf_ref[pl.ds(at + 1, 8, stride=pitch), :] = imag
+            leaf_ref[pl.ds(at + size, 8, stride=pitch), :] = imag
+            leaf_ref[pl.ds(at + size + 1, 8, stride=pitch), :] = real
+    for get in gets[:1] + gets[4:]:
+        get.wait()
     line = size + PAD
 
     def body(i, carry):
@@ -324,30 +361,31 @@
             out_ref[1, first:first + 8, lanes] = two_ref[even, :] + two_ref[odd, :]
 
 
-def leaf_translate(src, kind, own, low, high, table, after):
+def leaf_translate(src, kind, own, pair_a, pair_b, table, after):
     leaves = own.shape[1]
-    reach = low.shape[1]
+    reach = pair_a.shape[1]
     size = 2 * own.shape[2] // LANES
     line = size + PAD
+    near = leaves + 2 * reach
     return pl.pallas_call(
         leaf_kernel,
         out_shape=jax.ShapeDtypeStruct(own.shape, F32),
-        in_specs=[SMEM, SMEM, HBM, HBM, HBM, HBM, HBM],
+        in_specs=[HBM] * 7,
         out_specs=VMEM,
         scratch_shapes=[
-            pltpu.VMEM(own.shape, F32),
-            pltpu.VMEM(low.shape, F32),
-            pltpu.VMEM(high.shape, F32),
+            pltpu.SMEM(src.shape, I32),
+            pltpu.SMEM(kind.shape, I32),
+            pltpu.VMEM((2, near, own.shape[2]), F32),
             pltpu.VMEM(table.shape, F32),
-            pltpu.VMEM(((leaves + 2 * reach) * (2 * size + PAD), LANES), F32),
+            pltpu.VMEM((near * (2 * size + PAD), LANES), F32),
             pltpu.VMEM((leaves * line, LANES), F32),
             pltpu.VMEM((leaves * line, LANES), F32),
-            pltpu.SemaphoreType.DMA((4,)),
+            pltpu.SemaphoreType.DMA((6,)),
         ],
-        compiler_params=pltpu.CompilerParams(vmem_limit_bytes=40 * MIB),
+        compiler_params=pltpu.CompilerParams(vmem_limit_bytes=60 * MIB),
         cost_estimate=estimate(5),
         name="leaf_translate",
-    )(src, kind, own, low, high, table, after)
+    )(src, kind, own, pair_a, pair_b, table, after)
 
 
 def interleaved(table):
@@ -374,31 +412,30 @@
     dirs = lax.axis_size("dir")
     groups = lax.axis_size("box")
     box = lax.axis_index("box")
-    parents, low, high = aggregate(
+    parents, edge_b, edge_a = aggregate(
         leaf_pattern, octant, leaf_parent, interp_theta.T, interp_phi.T, shift_angle, dirs
     )
     directed = lax.all_to_all(parents, "dir", split_axis=0, concat_axis=0)
     count = dirs * groups
-    leaf_low = lax.ppermute(high, ("box", "dir"), [(i, i + 1) for i in range(count - 1)])
-    leaf_high = lax.ppermute(low, ("box", "dir"), [(i + 1, i) for i in range(count - 1)])
+    pair_a = lax.ppermute(edge_a, ("box", "dir"), [(i, i ^ 1) for i in range(count)])
+    pair_b = lax.ppermute(edge_b, ("box", "dir"), [(i, ((i + 1) ^ 1) - 1) for i in range(1, count - 1)])
 
     own = directed.reshape(-1, LANES)
     boxes = inter_src.shape[0]
     mate = lax.ppermute(own, "box", [(i, i ^ 1) for i in range(groups)])
     cross = lax.ppermute(own, "box", [(i, ((i + 1) ^ 1) - 1) for i in range(1, groups - 1)])
-    table = prepare(interleaved(top_transfer), low)
     src = inter_src.T
     group = src // boxes
     place = jnp.where(group == box, 0, jnp.where(group == (box ^ 1), boxes, 2 * boxes)) + src % boxes
     top_src = (place * 8).reshape(-1)
     top_type = (inter_type.T * 16).reshape(-1)
-    incoming = top_translate(top_src, top_type, own, mate, cross, table)
+    incoming = top_translate(top_src, top_type, own, mate, cross, interleaved(top_transfer))
 
     size = 2 * leaf_pattern.shape[2] // LANES
     first_leaf = lax.axis_index(("box", "dir")) * leaves
     leaf_src = (near_src.T - (first_leaf - REACH)) * (2 * size + PAD)
     leaf_incoming = leaf_translate(
-        leaf_src, near_type.T * size, leaf_pattern, leaf_low, leaf_high, interleaved(leaf_transfer), directed
+        leaf_src, near_type.T * size, leaf_pattern, pair_a, pair_b, interleaved(leaf_transfer), directed
     )
     return (incoming, leaf_incoming)
 

time: 67.3 us -> 53.2 us (0.79)
  the two profiles are of different devices: /device:TPU:1 before, /device:TPU:3 now
where the time goes in v1:
time: 53.2 us; the launch traced here: 52.7 us
  starting transfers between devices  23.1 us (43%)
  Pallas kernels  20.6 us (39%)
  waiting for transfers between devices  3.58 us (7%)
  other arithmetic  2.78 us (5%)
  local copies, waits for them, and re-layouts  1.83 us (3%)
  between operations  0.74 us (1%)
    pallas_call x1, Pallas kernels, top_translate(): pl.pallas_call(top_kernel, out_shape=jax.ShapeDtypeStruct((2, rows // 8,...  8.24 us
    all_to_all x1, starting transfers between devices, per_device(): directed = lax.all_to_all(parents, 'dir', split_axis=0, concat_axis=0)  7.78 us
    pallas_call x1, Pallas kernels, leaf_translate(): pl.pallas_call(leaf_kernel, out_shape=jax.ShapeDtypeStruct(own.shape, F32...  7.42 us
    ppermute x1, starting transfers between devices, per_device(): mate = lax.ppermute(own, 'box', [(i, i ^ 1) for i in range(groups)])  7.38 us
    pallas_call x1, Pallas kernels, aggregate(): pl.pallas_call(aggregate_kernel, out_shape=(jax.ShapeDtypeStruct((dirs, P...  4.99 us
    ppermute x1, starting transfers between devices, per_device(): lax.ppermute(edge_b, ('box', 'dir'), [(i, (i + 1 ^ 1) - 1) for i in range...  3.68 us
    all_to_all x1, waiting for transfers between devices, per_device(): directed = lax.all_to_all(parents, 'dir', split_axis=0, concat_axis=0)  3.57 us
    ppermute x1, starting transfers between devices, per_device(): lax.ppermute(own, 'box', [(i, (i + 1 ^ 1) - 1) for i in range(1, groups -...  3.09 us
  transfers between devices with their start and end apart: 5, of which 1 were waited for; matrix products, arithmetic and copies ran while one was open for 5% of the time, Pallas kernels for 14%

profile of v1, /device:TPU:3, one launch (start us, length us, event | category | flops | bytes accessed | tf_op | source)
XLA Modules:
  0.0 52.7 jit_solution(12404478570962174052)
XLA Ops:
  0.6 0.0 copy-start.2
  0.6 5.0 %aggregate.1 = (f32[16,64,128]{2,1,0:T(8,128)}, f32[2,16,2048]{2,1,0:T(8,128)}, f32[2,16,2048]{2,1,0:T(8,128)}) custom-call(s32[48]{0:T(128)} %oct_hbm.1, s32[1,48]{1,0:T(1,128)} %par_hbm.1, f32[2,48,2048]{2,1,0:T(8,128)} %own_hbm.1, f32[32,64]{1,0:T(8,128)} %bitcast.47, f32[64,128]{1,0:T(8,128)} %bitcast.46, f32[8,8192]{1,0:T(8,128)} %angle_hbm.1), custom_call_target="tpu_custom_call" | custom-call | flops 1000 | bytes 15000000 | tf_op jit(solution)/shard_map/aggregate/pallas_call | solution.py:184
  5.6 7.8 %all-to-all-start = ((f32[16,64,128]{2,1,0:T(8,128)}), f32[16,64,128]{2,1,0:T(8,128)S(1)}, u32[]{:S(2)}, u32[]{:S(2)}) async-start(f32[16,64,128]{2,1,0:T(8,128)} %get-tuple-element.5), calls=%async_computation | async-start | bytes 1048576 | tf_op jit(solution)/shard_map/all_to_all | solution.py:418
  13.4 1.2 %collective-permute-start.2 = (f32[2,16,2048]{2,1,0:T(8,128)}, f32[2,16,2048]{2,1,0:T(8,128)S(1)}, u32[]{:S(2)}, u32[]{:S(2)}) collective-permute-start(f32[2,16,2048]{2,1,0:T(8,128)} %get-tuple-element.6), channel_id=1, source_target_pairs={{0,1},{1,0},{2,3},{3,2},{4,5},{5,4},{6,7},{7,6},{8,9},{9,8},{10,11... | collective-permute-start | bytes 786440 | tf_op jit(solution)/shard_map/ppermute | solution.py:420
  14.6 3.7 %collective-permute-start.3 = (f32[2,16,2048]{2,1,0:T(8,128)}, f32[2,16,2048]{2,1,0:T(8,128)S(1)}, u32[]{:S(2)}, u32[]{:S(2)}) collective-permute-start(f32[2,16,2048]{2,1,0:T(8,128)} %get-tuple-element.7), channel_id=1, source_target_pairs={{1,2},{2,1},{3,4},{4,3},{5,6},{6,5},{7,8},{8,7},{9,10},{10,9},{11,... | collective-permute-start | bytes 786440 | tf_op jit(solution)/shard_map/ppermute | solution.py:421
  18.3 3.6 %all-to-all-done.after_hbm = f32[16,64,128]{2,1,0:T(8,128)S(1)} async-done(((f32[16,64,128]{2,1,0:T(8,128)}), f32[16,64,128]{2,1,0:T(8,128)S(1)}, u32[]{:S(2)}, u32[]{:S(2)}) %all-to-all-start) | async-done | bytes 524320 | tf_op jit(solution)/shard_map/all_to_all | solution.py:418
  21.9 0.0 copy-start
  21.9 7.4 %collective-permute-start = (f32[1024,128]{1,0:T(8,128)S(1)}, f32[1024,128]{1,0:T(8,128)S(1)}, u32[]{:S(2)}, u32[]{:S(2)}) collective-permute-start(f32[1024,128]{1,0:T(8,128)S(1)} %bitcast.41), channel_id=1, source_target_pairs={{0,16},{16,0},{32,48},{48,32},{64,80},{80,64},{96,112},{112,96},{1... | collective-permute-start | bytes 1572872 | tf_op jit(solution)/shard_map/ppermute | solution.py:425
  29.2 3.1 %collective-permute-start.1 = (f32[1024,128]{1,0:T(8,128)S(1)}, f32[1024,128]{1,0:T(8,128)S(1)}, u32[]{:S(2)}, u32[]{:S(2)}) collective-permute-start(f32[1024,128]{1,0:T(8,128)S(1)} %bitcast.42), channel_id=1, source_target_pairs={{16,32},{32,16},{48,64},{64,48},{80,96},{96,80},{17,33},{33,17},{4... | collective-permute-start | bytes 1572872 | tf_op jit(solution)/shard_map/ppermute | solution.py:426
  32.3 0.7 %multiply_bitcast_fusion.type_ref = s32[4096]{0:T(1024)S(1)} fusion(s32[128,32]{0,1:T(8,128)} %param.22), kind=kLoop, calls=%fused_computation.11 | loop fusion | flops 4096 | bytes 32768 | tf_op jit(solution)/shard_map/reshape | solution.py:431
  33.1 0.7 %fusion.2.src_ref = s32[4096]{0:T(1024)S(1)} fusion(s32[128,32]{0,1:T(8,128)} %param.21, s32[]{:T(128)S(6)} %xor.3, s32[]{:T(128)S(6)} %axis_index.27), kind=kLoop, calls=%fused_computation.7 | loop fusion | flops 102400 | bytes 32776 | tf_op jit(solution)/shard_map/reshape | solution.py:430
  33.8 1.3 %multiply_bitcast_fusion.1 = (s32[16,48]{1,0:T(8,128)}, s32[16,48]{1,0:T(8,128)}) fusion(s32[48,16]{0,1:T(8,128)} %param.19, s32[48,16]{0,1:T(8,128)} %param.18, s32[]{:T(128)S(6)} %sub.17), kind=kLoop, calls=%fused_computation.13 | loop fusion | flops 2304 | bytes 12292 | tf_op jit(solution)/shard_map/mul | solution.py:438
  35.1 0.0 collective-permute-done.2.pair_a_hbm
  35.1 0.0 copy-start.3
  35.1 0.0 collective-permute-done.3.pair_b_hbm
  35.1 0.0 copy-start.4
  35.2 0.0 copy-done
  35.2 0.7 %copy-done.3 = f32[2,16,2048]{2,1,0:T(8,128)} copy-done((f32[2,16,2048]{2,1,0:T(8,128)}, f32[2,16,2048]{2,1,0:T(8,128)S(1)}, u32[]{:S(2)}) %copy-start.3) | copy-done | bytes 262168
  35.8 0.1 copy-done.4
  35.9 7.4 %leaf_translate.1 = f32[2,48,2048]{2,1,0:T(8,128)} custom-call(s32[16,48]{1,0:T(8,128)} %get-tuple-element.9.src_hbm, s32[16,48]{1,0:T(8,128)} %get-tuple-element.8.type_hbm, f32[2,48,2048]{2,1,0:T(8,128)} %own_hbm.1, f32[2,16,2048]{2,1,0:T(8,128)} %copy-done.3, f32[2,16,2048]{2,1,0:T(8,128)} %copy-done.4, f32[10112,128]{1,0:T(8,128)} %bitcast.45, ...), custom_call_target="tpu_custom_call" | custom-call | flops 1000 | bytes 15000000 | tf_op jit(solution)/shard_map/leaf_translate/pallas_call | solution.py:370
  43.4 0.0 collective-permute-done.mate_hbm
  43.4 0.0 collective-permute-done.1.cross_hbm
  43.4 0.0 copy-done.2
  43.4 0.0 copy-start.1
  43.4 1.0 %copy-done.1 = f32[16,64,128]{2,1,0:T(8,128)S(1)} copy-done((f32[16,64,128]{2,1,0:T(8,128)S(1)}, f32[16,64,128]{2,1,0:T(8,128)}, u32[]{:S(2)}) %copy-start.1) | copy-done | bytes 524312
  44.4 8.2 %top_translate.1 = f32[2,128,512]{2,1,0:T(8,128)} custom-call(s32[4096]{0:T(1024)S(1)} %fusion.2.src_ref, s32[4096]{0:T(1024)S(1)} %multiply_bitcast_fusion.type_ref, f32[1024,128]{1,0:T(8,128)S(1)} %bitcast.43, f32[1024,128]{1,0:T(8,128)S(1)} %collective-permute-done.mate_hbm, f32[1024,128]{1,0:T(8,128)S(1)} %collective-permute-done.1.cross_hbm, ...), custom_call_target="tpu_custom_call" | custom-call | flops 1000 | bytes 27000000 | tf_op jit(solution)/shard_map/top_translate/pallas_call | solution.py:263
Async XLA Ops:
  0.6 42.8 %copy-start.2 = (f32[2,316,512]{2,0,1:T(2,128)S(1)}, f32[2,316,512]{2,0,1:T(2,128)}, u32[]{:S(2)}) copy-start(f32[2,316,512]{2,0,1:T(2,128)} %param.23) | copy-start | bytes 3883012
  5.6 16.2 %all-to-all-start = ((f32[16,64,128]{2,1,0:T(8,128)}), f32[16,64,128]{2,1,0:T(8,128)S(1)}, u32[]{:S(2)}, u32[]{:S(2)}) async-start(f32[16,64,128]{2,1,0:T(8,128)} %get-tuple-element.5), calls=%async_computation | async-start | bytes 1048576 | tf_op jit(solution)/shard_map/all_to_all | solution.py:418
  13.4 21.7 %collective-permute-start.2 = (f32[2,16,2048]{2,1,0:T(8,128)}, f32[2,16,2048]{2,1,0:T(8,128)S(1)}, u32[]{:S(2)}, u32[]{:S(2)}) collective-permute-start(f32[2,16,2048]{2,1,0:T(8,128)} %get-tuple-element.6), channel_id=1, source_target_pairs={{0,1},{1,0},{2,3},{3,2},{4,5},{5,4},{6,7},{7,6},{8,9},{9,8},{10,11... | collective-permute-start | bytes 786440 | tf_op jit(solution)/shard_map/ppermute | solution.py:420
  14.6 20.5 %collective-permute-start.3 = (f32[2,16,2048]{2,1,0:T(8,128)}, f32[2,16,2048]{2,1,0:T(8,128)S(1)}, u32[]{:S(2)}, u32[]{:S(2)}) collective-permute-start(f32[2,16,2048]{2,1,0:T(8,128)} %get-tuple-element.7), channel_id=1, source_target_pairs={{1,2},{2,1},{3,4},{4,3},{5,6},{6,5},{7,8},{8,7},{9,10},{10,9},{11,... | collective-permute-start | bytes 786440 | tf_op jit(solution)/shard_map/ppermute | solution.py:421
  21.9 13.3 %copy-start = (f32[16,64,128]{2,1,0:T(8,128)}, f32[16,64,128]{2,1,0:T(8,128)S(1)}, u32[]{:S(2)}) copy-start(f32[16,64,128]{2,1,0:T(8,128)S(1)} %all-to-all-done.after_hbm) | copy-start | bytes 1572868
  21.9 21.5 %collective-permute-start = (f32[1024,128]{1,0:T(8,128)S(1)}, f32[1024,128]{1,0:T(8,128)S(1)}, u32[]{:S(2)}, u32[]{:S(2)}) collective-permute-start(f32[1024,128]{1,0:T(8,128)S(1)} %bitcast.41), channel_id=1, source_target_pairs={{0,16},{16,0},{32,48},{48,32},{64,80},{80,64},{96,112},{112,96},{1... | collective-permute-start | bytes 1572872 | tf_op jit(solution)/shard_map/ppermute | solution.py:425
  29.2 14.1 %collective-permute-start.1 = (f32[1024,128]{1,0:T(8,128)S(1)}, f32[1024,128]{1,0:T(8,128)S(1)}, u32[]{:S(2)}, u32[]{:S(2)}) collective-permute-start(f32[1024,128]{1,0:T(8,128)S(1)} %bitcast.42), channel_id=1, source_target_pairs={{16,32},{32,16},{48,64},{64,48},{80,96},{96,80},{17,33},{33,17},{4... | collective-permute-start | bytes 1572872 | tf_op jit(solution)/shard_map/ppermute | solution.py:426
  35.1 0.7 %copy-start.3 = (f32[2,16,2048]{2,1,0:T(8,128)}, f32[2,16,2048]{2,1,0:T(8,128)S(1)}, u32[]{:S(2)}) copy-start(f32[2,16,2048]{2,1,0:T(8,128)S(1)} %collective-permute-done.2.pair_a_hbm) | copy-start | bytes 786436
  35.1 0.8 %copy-start.4 = (f32[2,16,2048]{2,1,0:T(8,128)}, f32[2,16,2048]{2,1,0:T(8,128)S(1)}, u32[]{:S(2)}) copy-start(f32[2,16,2048]{2,1,0:T(8,128)S(1)} %collective-permute-done.3.pair_b_hbm) | copy-start | bytes 786436
  43.4 1.0 %copy-start.1 = (f32[16,64,128]{2,1,0:T(8,128)S(1)}, f32[16,64,128]{2,1,0:T(8,128)}, u32[]{:S(2)}) copy-start(f32[16,64,128]{2,1,0:T(8,128)} %copy-done) | copy-start | bytes 1572868

commit v2 on v1

--- a/solution.py
+++ b/solution.py
@@ -20,6 +20,7 @@
 VMEM = pl.BlockSpec(memory_space=pltpu.VMEM)
 SMEM = pl.BlockSpec(memory_space=pltpu.SMEM)
 HBM = pl.BlockSpec(memory_space=pltpu.HBM)
+ANY = pl.BlockSpec(memory_space=pl.ANY)
 
 
 def split(x):
@@ -205,7 +206,7 @@
 
 
 def top_kernel(
-    src_ref, type_ref, own_hbm, mate_hbm, cross_hbm, table_hbm, out_ref, box_ref, table_ref, tab_ref, one_ref, two_ref, sem
+    src_ref, type_ref, own_hbm, mate_hbm, cross_hbm, table_hbm, out_hbm, out_ref, box_ref, table_ref, tab_ref, one_ref, two_ref, sem
 ):
     span = own_hbm.shape[0]
     boxes = span // 8
@@ -248,14 +249,24 @@
             two_ref[at, :] = two[k]
         return carry
 
-    lax.fori_loop(0, boxes // together, body, 0)
-    for r in range(0, boxes, 8):
-        for c in range(4):
-            lanes = slice(c * LANES, (c + 1) * LANES)
-            even = pl.ds(8 * r + 2 * c, 8, stride=8)
-            odd = pl.ds(8 * r + 2 * c + 1, 8, stride=8)
-            out_ref[0, r:r + 8, lanes] = one_ref[even, :] - one_ref[odd, :]
-            out_ref[1, r:r + 8, lanes] = two_ref[even, :] + two_ref[odd, :]
+    steps = boxes // together
+    parts = 4
+    puts = []
+    for q in range(parts):
+        lax.fori_loop(q * steps // parts, (q + 1) * steps // parts, body, 0)
+        start = q * boxes // parts
+        for r in range(start, start + boxes // parts, 8):
+            for c in range(4):
+                lanes = slice(c * LANES, (c + 1) * LANES)
+                even = pl.ds(8 * r + 2 * c, 8, stride=8)
+                odd = pl.ds(8 * r + 2 * c + 1, 8, stride=8)
+                out_ref[0, r:r + 8, lanes] = one_ref[even, :] - one_ref[odd, :]
+                out_ref[1, r:r + 8, lanes] = two_ref[even, :] + two_ref[odd, :]
+        rows = slice(start, start + boxes // parts)
+        puts.append(pltpu.make_async_copy(out_ref.at[:, rows, :], out_hbm.at[:, rows, :], sem.at[4 + q]))
+        puts[q].start()
+    for put in puts:
+        put.wait()
 
 
 def top_translate(src, kind, own, mate, cross, table):
@@ -264,14 +275,15 @@
         top_kernel,
         out_shape=jax.ShapeDtypeStruct((2, rows // 8, 4 * LANES), F32),
         in_specs=[SMEM, SMEM, HBM, HBM, HBM, HBM],
-        out_specs=VMEM,
+        out_specs=HBM,
         scratch_shapes=[
+            pltpu.VMEM((2, rows // 8, 4 * LANES), F32),
             pltpu.VMEM((3 * rows, LANES), F32),
             pltpu.VMEM(table.shape, F32),
             pltpu.VMEM((2 * table.shape[0], LANES), F32),
             pltpu.VMEM((rows, LANES), F32),
             pltpu.VMEM((rows, LANES), F32),
-            pltpu.SemaphoreType.DMA((4,)),
+            pltpu.SemaphoreType.DMA((8,)),
         ],
         compiler_params=pltpu.CompilerParams(vmem_limit_bytes=24 * MIB),
         cost_estimate=estimate(9),
@@ -286,7 +298,7 @@
     pair_a_hbm,
     pair_b_hbm,
     table_hbm,
-    after_hbm,
+    out_hbm,
     out_ref,
     src_ref,
     type_ref,
@@ -302,10 +314,10 @@
     chunks = own_hbm.shape[2] // LANES
     size = 2 * chunks
     pitch = 2 * size + PAD
-    odd = lax.axis_index("dir") % 2
+    side = lax.axis_index("dir") % 2
     after = reach + leaves
-    place_a = pl.multiple_of((1 - odd) * after, 8)
-    place_b = pl.multiple_of(odd * after, 8)
+    place_a = pl.multiple_of((1 - side) * after, 8)
+    place_b = pl.multiple_of(side * after, 8)
     gets = [
         pltpu.make_async_copy(source, target, sem.at[i])
         for i, (source, target) in enumerate(
@@ -351,17 +363,26 @@
         two_ref[at, :] = two
         return carry
 
-    lax.fori_loop(0, leaves, body, 0)
-    for first in range(0, leaves, 8):
-        for c in range(chunks):
-            lanes = slice(c * LANES, (c + 1) * LANES)
-            even = pl.ds(first * line + 2 * c, 8, stride=line)
-            odd = pl.ds(first * line + 2 * c + 1, 8, stride=line)
-            out_ref[0, first:first + 8, lanes] = one_ref[even, :] - one_ref[odd, :]
-            out_ref[1, first:first + 8, lanes] = two_ref[even, :] + two_ref[odd, :]
-
-
-def leaf_translate(src, kind, own, pair_a, pair_b, table, after):
+    parts = 3
+    puts = []
+    for q in range(parts):
+        start = q * leaves // parts
+        rows = slice(start, start + leaves // parts)
+        lax.fori_loop(rows.start, rows.stop, body, 0)
+        for first in range(rows.start, rows.stop, 8):
+            for c in range(chunks):
+                lanes = slice(c * LANES, (c + 1) * LANES)
+                even = pl.ds(first * line + 2 * c, 8, stride=line)
+                odd = pl.ds(first * line + 2 * c + 1, 8, stride=line)
+                out_ref[0, first:first + 8, lanes] = one_ref[even, :] - one_ref[odd, :]
+                out_ref[1, first:first + 8, lanes] = two_ref[even, :] + two_ref[odd, :]
+        puts.append(pltpu.make_async_copy(out_ref.at[:, rows, :], out_hbm.at[:, rows, :], sem.at[6 + q]))
+        puts[q].start()
+    for put in puts:
+        put.wait()
+
+
+def leaf_translate(src, kind, own, pair_a, pair_b, table):
     leaves = own.shape[1]
     reach = pair_a.shape[1]
     size = 2 * own.shape[2] // LANES
@@ -370,9 +391,10 @@
     return pl.pallas_call(
         leaf_kernel,
         out_shape=jax.ShapeDtypeStruct(own.shape, F32),
-        in_specs=[HBM] * 7,
-        out_specs=VMEM,
+        in_specs=[ANY, ANY, HBM, ANY, ANY, HBM],
+        out_specs=HBM,
         scratch_shapes=[
+            pltpu.VMEM(own.shape, F32),
             pltpu.SMEM(src.shape, I32),
             pltpu.SMEM(kind.shape, I32),
             pltpu.VMEM((2, near, own.shape[2]), F32),
@@ -380,12 +402,12 @@
             pltpu.VMEM((near * (2 * size + PAD), LANES), F32),
             pltpu.VMEM((leaves * line, LANES), F32),
             pltpu.VMEM((leaves * line, LANES), F32),
-            pltpu.SemaphoreType.DMA((6,)),
+            pltpu.SemaphoreType.DMA((9,)),
         ],
-        compiler_params=pltpu.CompilerParams(vmem_limit_bytes=60 * MIB),
+        compiler_params=pltpu.CompilerParams(vmem_limit_bytes=53 * MIB),
         cost_estimate=estimate(5),
         name="leaf_translate",
-    )(src, kind, own, pair_a, pair_b, table, after)
+    )(src, kind, own, pair_a, pair_b, table)
 
 
 def interleaved(table):
@@ -435,7 +457,7 @@
     first_leaf = lax.axis_index(("box", "dir")) * leaves
     leaf_src = (near_src.T - (first_leaf - REACH)) * (2 * size + PAD)
     leaf_incoming = leaf_translate(
-        leaf_src, near_type.T * size, leaf_pattern, pair_a, pair_b, interleaved(leaf_transfer), directed
+        leaf_src, near_type.T * size, leaf_pattern, pair_a, pair_b, interleaved(leaf_transfer)
     )
     return (incoming, leaf_incoming)
 

time: 53.2 us -> 50.4 us (0.947)
  local copies, waits for them, and re-layouts: 1.83 us -> 0.01 us
  other arithmetic: 2.78 us -> 2.18 us
    unnamed x10 -> x2, local copies, waits for them, and re-layouts: 1.83 us -> 0.01 us
    mul x1, other arithmetic: 1.32 us -> 0.72 us  [per_device(): near_type.T * size]
  transfers between devices with their start and end apart: 5 -> 5, of which waited for: 1 -> 1; matrix products, arithmetic and copies ran while one was open for 5% -> 4% of each run, Pallas kernels for 14% -> 14%
where the time goes in v2:
time: 50.4 us; the launch traced here: 49.9 us
  starting transfers between devices  23.1 us (46%)
  Pallas kernels  20.3 us (40%)
  waiting for transfers between devices  3.55 us (7%)
  other arithmetic  2.18 us (4%)
  between operations  0.71 us (1%)
    pallas_call x1, Pallas kernels, top_translate(): pl.pallas_call(top_kernel, out_shape=jax.ShapeDtypeStruct((2, rows // 8,...  8.14 us
    all_to_all x1, starting transfers between devices, per_device(): directed = lax.all_to_all(parents, 'dir', split_axis=0, concat_axis=0)  7.75 us
    ppermute x1, starting transfers between devices, per_device(): mate = lax.ppermute(own, 'box', [(i, i ^ 1) for i in range(groups)])  7.4 us
    pallas_call x1, Pallas kernels, leaf_translate(): pl.pallas_call(leaf_kernel, out_shape=jax.ShapeDtypeStruct(own.shape, F32...  7.15 us
    pallas_call x1, Pallas kernels, aggregate(): pl.pallas_call(aggregate_kernel, out_shape=(jax.ShapeDtypeStruct((dirs, P...  4.99 us
    ppermute x1, starting transfers between devices, per_device(): lax.ppermute(edge_b, ('box', 'dir'), [(i, (i + 1 ^ 1) - 1) for i in range...  3.68 us
    all_to_all x1, waiting for transfers between devices, per_device(): directed = lax.all_to_all(parents, 'dir', split_axis=0, concat_axis=0)  3.54 us
    ppermute x1, starting transfers between devices, per_device(): lax.ppermute(own, 'box', [(i, (i + 1 ^ 1) - 1) for i in range(1, groups -...  3.09 us
  transfers between devices with their start and end apart: 5, of which 1 were waited for; matrix products, arithmetic and copies ran while one was open for 4% of the time, Pallas kernels for 14%

profile of v2, /device:TPU:3, one launch (start us, length us, event | category | flops | bytes accessed | tf_op | source)
XLA Modules:
  0.0 49.9 jit_solution(15099776196474235611)
XLA Ops:
  0.6 0.0 copy-start
  0.6 5.0 %aggregate.1 = (f32[16,64,128]{2,1,0:T(8,128)}, f32[2,16,2048]{2,1,0:T(8,128)}, f32[2,16,2048]{2,1,0:T(8,128)}) custom-call(s32[48]{0:T(128)} %oct_hbm.1, s32[1,48]{1,0:T(1,128)} %par_hbm.1, f32[2,48,2048]{2,1,0:T(8,128)} %own_hbm.1, f32[32,64]{1,0:T(8,128)} %bitcast.47, f32[64,128]{1,0:T(8,128)} %bitcast.46, f32[8,8192]{1,0:T(8,128)} %angle_hbm.1), custom_call_target="tpu_custom_call" | custom-call | flops 1000 | bytes 15000000 | tf_op jit(solution)/shard_map/aggregate/pallas_call | solution.py:185
  5.6 7.7 %all-to-all-start = ((f32[16,64,128]{2,1,0:T(8,128)}), f32[16,64,128]{2,1,0:T(8,128)S(1)}, u32[]{:S(2)}, u32[]{:S(2)}) async-start(f32[16,64,128]{2,1,0:T(8,128)} %get-tuple-element.5), calls=%async_computation | async-start | bytes 1048576 | tf_op jit(solution)/shard_map/all_to_all | solution.py:440
  13.4 1.2 %collective-permute-start.2 = (f32[2,16,2048]{2,1,0:T(8,128)}, f32[2,16,2048]{2,1,0:T(8,128)S(1)}, u32[]{:S(2)}, u32[]{:S(2)}) collective-permute-start(f32[2,16,2048]{2,1,0:T(8,128)} %get-tuple-element.6), channel_id=1, source_target_pairs={{0,1},{1,0},{2,3},{3,2},{4,5},{5,4},{6,7},{7,6},{8,9},{9,8},{10,11... | collective-permute-start | bytes 786440 | tf_op jit(solution)/shard_map/ppermute | solution.py:442
  14.6 3.7 %collective-permute-start.3 = (f32[2,16,2048]{2,1,0:T(8,128)}, f32[2,16,2048]{2,1,0:T(8,128)S(1)}, u32[]{:S(2)}, u32[]{:S(2)}) collective-permute-start(f32[2,16,2048]{2,1,0:T(8,128)} %get-tuple-element.7), channel_id=1, source_target_pairs={{1,2},{2,1},{3,4},{4,3},{5,6},{6,5},{7,8},{8,7},{9,10},{10,9},{11,... | collective-permute-start | bytes 786440 | tf_op jit(solution)/shard_map/ppermute | solution.py:443
  18.3 3.5 %all-to-all-done = f32[16,64,128]{2,1,0:T(8,128)S(1)} async-done(((f32[16,64,128]{2,1,0:T(8,128)}), f32[16,64,128]{2,1,0:T(8,128)S(1)}, u32[]{:S(2)}, u32[]{:S(2)}) %all-to-all-start) | async-done | bytes 524320 | tf_op jit(solution)/shard_map/all_to_all | solution.py:440
  21.8 7.4 %collective-permute-start = (f32[1024,128]{1,0:T(8,128)S(1)}, f32[1024,128]{1,0:T(8,128)S(1)}, u32[]{:S(2)}, u32[]{:S(2)}) collective-permute-start(f32[1024,128]{1,0:T(8,128)S(1)} %bitcast.41), channel_id=1, source_target_pairs={{0,16},{16,0},{32,48},{48,32},{64,80},{80,64},{96,112},{112,96},{1... | collective-permute-start | bytes 1572872 | tf_op jit(solution)/shard_map/ppermute | solution.py:447
  29.2 3.1 %collective-permute-start.1 = (f32[1024,128]{1,0:T(8,128)S(1)}, f32[1024,128]{1,0:T(8,128)S(1)}, u32[]{:S(2)}, u32[]{:S(2)}) collective-permute-start(f32[1024,128]{1,0:T(8,128)S(1)} %bitcast.42), channel_id=1, source_target_pairs={{16,32},{32,16},{48,64},{64,48},{80,96},{96,80},{17,33},{33,17},{4... | collective-permute-start | bytes 1572872 | tf_op jit(solution)/shard_map/ppermute | solution.py:448
  32.3 0.7 %multiply_bitcast_fusion.type_ref = s32[4096]{0:T(1024)S(1)} fusion(s32[128,32]{0,1:T(8,128)} %param.22), kind=kLoop, calls=%fused_computation.11 | loop fusion | flops 4096 | bytes 32768 | tf_op jit(solution)/shard_map/reshape | solution.py:453
  33.0 0.7 %fusion.2.src_ref = s32[4096]{0:T(1024)S(1)} fusion(s32[128,32]{0,1:T(8,128)} %param.21, s32[]{:T(128)S(6)} %xor.3, s32[]{:T(128)S(6)} %axis_index.27), kind=kLoop, calls=%fused_computation.7 | loop fusion | flops 102400 | bytes 32776 | tf_op jit(solution)/shard_map/reshape | solution.py:452
  33.8 0.7 %multiply_bitcast_fusion.1 = (s32[16,48]{1,0:T(8,128)S(1)}, s32[16,48]{1,0:T(8,128)S(1)}) fusion(s32[48,16]{0,1:T(8,128)} %param.19, s32[48,16]{0,1:T(8,128)} %param.18, s32[]{:T(128)S(6)} %sub.17), kind=kLoop, calls=%fused_computation.13 | loop fusion | flops 2304 | bytes 12292 | tf_op jit(solution)/shard_map/mul | solution.py:460
  34.5 0.0 collective-permute-done.2.pair_a_hbm
  34.5 0.0 collective-permute-done.3.pair_b_hbm
  34.5 7.2 %leaf_translate.1 = f32[2,48,2048]{2,1,0:T(8,128)} custom-call(s32[16,48]{1,0:T(8,128)S(1)} %get-tuple-element.9.src_hbm, s32[16,48]{1,0:T(8,128)S(1)} %get-tuple-element.8.type_hbm, f32[2,48,2048]{2,1,0:T(8,128)} %own_hbm.1, f32[2,16,2048]{2,1,0:T(8,128)S(1)} %collective-permute-done.2.pair_a_hbm, f32[2,16,2048]{2,1,0:T(8,128)S(1)} %collective-permute-done.3.pair_b_hbm, ...), custom_call_target="tpu_custom_call" | custom-call | flops 1000 | bytes 15000000 | tf_op jit(solution)/shard_map/leaf_translate/pallas_call | solution.py:391
  41.7 0.0 collective-permute-done.mate_hbm
  41.7 0.0 collective-permute-done.1.cross_hbm
  41.7 0.0 copy-done
  41.7 8.1 %top_translate.1 = f32[2,128,512]{2,1,0:T(8,128)} custom-call(s32[4096]{0:T(1024)S(1)} %fusion.2.src_ref, s32[4096]{0:T(1024)S(1)} %multiply_bitcast_fusion.type_ref, f32[1024,128]{1,0:T(8,128)S(1)} %bitcast.43, f32[1024,128]{1,0:T(8,128)S(1)} %collective-permute-done.mate_hbm, f32[1024,128]{1,0:T(8,128)S(1)} %collective-permute-done.1.cross_hbm, ...), custom_call_target="tpu_custom_call" | custom-call | flops 1000 | bytes 27000000 | tf_op jit(solution)/shard_map/top_translate/pallas_call | solution.py:274
Async XLA Ops:
  0.6 41.1 %copy-start = (f32[2,316,512]{2,0,1:T(2,128)S(1)}, f32[2,316,512]{2,0,1:T(2,128)}, u32[]{:S(2)}) copy-start(f32[2,316,512]{2,0,1:T(2,128)} %param.23) | copy-start | bytes 3883012
  5.6 16.2 %all-to-all-start = ((f32[16,64,128]{2,1,0:T(8,128)}), f32[16,64,128]{2,1,0:T(8,128)S(1)}, u32[]{:S(2)}, u32[]{:S(2)}) async-start(f32[16,64,128]{2,1,0:T(8,128)} %get-tuple-element.5), calls=%async_computation | async-start | bytes 1048576 | tf_op jit(solution)/shard_map/all_to_all | solution.py:440
  13.4 21.1 %collective-permute-start.2 = (f32[2,16,2048]{2,1,0:T(8,128)}, f32[2,16,2048]{2,1,0:T(8,128)S(1)}, u32[]{:S(2)}, u32[]{:S(2)}) collective-permute-start(f32[2,16,2048]{2,1,0:T(8,128)} %get-tuple-element.6), channel_id=1, source_target_pairs={{0,1},{1,0},{2,3},{3,2},{4,5},{5,4},{6,7},{7,6},{8,9},{9,8},{10,11... | collective-permute-start | bytes 786440 | tf_op jit(solution)/shard_map/ppermute | solution.py:442
  14.6 19.9 %collective-permute-start.3 = (f32[2,16,2048]{2,1,0:T(8,128)}, f32[2,16,2048]{2,1,0:T(8,128)S(1)}, u32[]{:S(2)}, u32[]{:S(2)}) collective-permute-start(f32[2,16,2048]{2,1,0:T(8,128)} %get-tuple-element.7), channel_id=1, source_target_pairs={{1,2},{2,1},{3,4},{4,3},{5,6},{6,5},{7,8},{8,7},{9,10},{10,9},{11,... | collective-permute-start | bytes 786440 | tf_op jit(solution)/shard_map/ppermute | solution.py:443
  21.8 19.9 %collective-permute-start = (f32[1024,128]{1,0:T(8,128)S(1)}, f32[1024,128]{1,0:T(8,128)S(1)}, u32[]{:S(2)}, u32[]{:S(2)}) collective-permute-start(f32[1024,128]{1,0:T(8,128)S(1)} %bitcast.41), channel_id=1, source_target_pairs={{0,16},{16,0},{32,48},{48,32},{64,80},{80,64},{96,112},{112,96},{1... | collective-permute-start | bytes 1572872 | tf_op jit(solution)/shard_map/ppermute | solution.py:447
  29.2 12.5 %collective-permute-start.1 = (f32[1024,128]{1,0:T(8,128)S(1)}, f32[1024,128]{1,0:T(8,128)S(1)}, u32[]{:S(2)}, u32[]{:S(2)}) collective-permute-start(f32[1024,128]{1,0:T(8,128)S(1)} %bitcast.42), channel_id=1, source_target_pairs={{16,32},{32,16},{48,64},{64,48},{80,96},{96,80},{17,33},{33,17},{4... | collective-permute-start | bytes 1572872 | tf_op jit(solution)/shard_map/ppermute | solution.py:448

commit v3 on v2

--- a/solution.py
+++ b/solution.py
@@ -322,7 +322,6 @@
         pltpu.make_async_copy(source, target, sem.at[i])
         for i, (source, target) in enumerate(
             (
-                (table_hbm, tab_ref),
                 (own_hbm, near_ref.at[:, reach:after, :]),
                 (pair_a_hbm, near_ref.at[:, pl.ds(place_a, reach), :]),
                 (pair_b_hbm, near_ref.at[:, pl.ds(place_b, reach), :]),
@@ -331,9 +330,16 @@
             )
         )
     ]
-    for get in gets:
+    share = table_hbm.shape[0] // 4
+    tables = [
+        pltpu.make_async_copy(
+            table_hbm.at[q * share:(q + 1) * share, :], tab_ref.at[q * share:(q + 1) * share, :], sem.at[8 + q]
+        )
+        for q in range(4)
+    ]
+    for get in gets[:3] + tables + gets[3:]:
         get.start()
-    for get in gets[1:4]:
+    for get in gets[:3]:
         get.wait()
     for first in range(0, near_ref.shape[1], 8):
         for c in range(chunks):
@@ -345,7 +351,7 @@
             leaf_ref[pl.ds(at + 1, 8, stride=pitch), :] = imag
             leaf_ref[pl.ds(at + size, 8, stride=pitch), :] = imag
             leaf_ref[pl.ds(at + size + 1, 8, stride=pitch), :] = real
-    for get in gets[:1] + gets[4:]:
+    for get in tables + gets[3:]:
         get.wait()
     line = size + PAD
 
@@ -376,7 +382,7 @@
                 odd = pl.ds(first * line + 2 * c + 1, 8, stride=line)
                 out_ref[0, first:first + 8, lanes] = one_ref[even, :] - one_ref[odd, :]
                 out_ref[1, first:first + 8, lanes] = two_ref[even, :] + two_ref[odd, :]
-        puts.append(pltpu.make_async_copy(out_ref.at[:, rows, :], out_hbm.at[:, rows, :], sem.at[6 + q]))
+        puts.append(pltpu.make_async_copy(out_ref.at[:, rows, :], out_hbm.at[:, rows, :], sem.at[5 + q]))
         puts[q].start()
     for put in puts:
         put.wait()
@@ -402,7 +408,7 @@
             pltpu.VMEM((near * (2 * size + PAD), LANES), F32),
             pltpu.VMEM((leaves * line, LANES), F32),
             pltpu.VMEM((leaves * line, LANES), F32),
-            pltpu.SemaphoreType.DMA((9,)),
+            pltpu.SemaphoreType.DMA((12,)),
         ],
         compiler_params=pltpu.CompilerParams(vmem_limit_bytes=53 * MIB),
         cost_estimate=estimate(5),

time: 50.4 us -> 50.1 us (level)
  no operation moved by 1% of the time
where the time goes in v3:
time: 50.1 us; the launch traced here: 49.6 us
  starting transfers between devices  23.1 us (46%)
  Pallas kernels  20 us (40%)
  waiting for transfers between devices  3.59 us (7%)
  other arithmetic  2.18 us (4%)
  between operations  0.71 us (1%)
    pallas_call x1, Pallas kernels, top_translate(): pl.pallas_call(top_kernel, out_shape=jax.ShapeDtypeStruct((2, rows // 8,...  8.14 us
    all_to_all x1, starting transfers between devices, per_device(): directed = lax.all_to_all(parents, 'dir', split_axis=0, concat_axis=0)  7.76 us
    ppermute x1, starting transfers between devices, per_device(): mate = lax.ppermute(own, 'box', [(i, i ^ 1) for i in range(groups)])  7.37 us
    pallas_call x1, Pallas kernels, leaf_translate(): pl.pallas_call(leaf_kernel, out_shape=jax.ShapeDtypeStruct(own.shape, F32...  6.86 us
    pallas_call x1, Pallas kernels, aggregate(): pl.pallas_call(aggregate_kernel, out_shape=(jax.ShapeDtypeStruct((dirs, P...  4.99 us
    ppermute x1, starting transfers between devices, per_device(): lax.ppermute(edge_b, ('box', 'dir'), [(i, (i + 1 ^ 1) - 1) for i in range...  3.68 us
    all_to_all x1, waiting for transfers between devices, per_device(): directed = lax.all_to_all(parents, 'dir', split_axis=0, concat_axis=0)  3.57 us
    ppermute x1, starting transfers between devices, per_device(): lax.ppermute(own, 'box', [(i, (i + 1 ^ 1) - 1) for i in range(1, groups -...  3.09 us
  transfers between devices with their start and end apart: 5, of which 1 were waited for; matrix products, arithmetic and copies ran while one was open for 4% of the time, Pallas kernels for 14%

profile of v3, /device:TPU:3, one launch (start us, length us, event | category | flops | bytes accessed | tf_op | source)
XLA Modules:
  0.0 49.6 jit_solution(811067895700590444)
XLA Ops:
  0.6 0.0 copy-start
  0.6 5.0 %aggregate.1 = (f32[16,64,128]{2,1,0:T(8,128)}, f32[2,16,2048]{2,1,0:T(8,128)}, f32[2,16,2048]{2,1,0:T(8,128)}) custom-call(s32[48]{0:T(128)} %oct_hbm.1, s32[1,48]{1,0:T(1,128)} %par_hbm.1, f32[2,48,2048]{2,1,0:T(8,128)} %own_hbm.1, f32[32,64]{1,0:T(8,128)} %bitcast.47, f32[64,128]{1,0:T(8,128)} %bitcast.46, f32[8,8192]{1,0:T(8,128)} %angle_hbm.1), custom_call_target="tpu_custom_call" | custom-call | flops 1000 | bytes 15000000 | tf_op jit(solution)/shard_map/aggregate/pallas_call | solution.py:185
  5.6 7.8 %all-to-all-start = ((f32[16,64,128]{2,1,0:T(8,128)}), f32[16,64,128]{2,1,0:T(8,128)S(1)}, u32[]{:S(2)}, u32[]{:S(2)}) async-start(f32[16,64,128]{2,1,0:T(8,128)} %get-tuple-element.5), calls=%async_computation | async-start | bytes 1048576 | tf_op jit(solution)/shard_map/all_to_all | solution.py:446
  13.4 1.2 %collective-permute-start.2 = (f32[2,16,2048]{2,1,0:T(8,128)}, f32[2,16,2048]{2,1,0:T(8,128)S(1)}, u32[]{:S(2)}, u32[]{:S(2)}) collective-permute-start(f32[2,16,2048]{2,1,0:T(8,128)} %get-tuple-element.6), channel_id=1, source_target_pairs={{0,1},{1,0},{2,3},{3,2},{4,5},{5,4},{6,7},{7,6},{8,9},{9,8},{10,11... | collective-permute-start | bytes 786440 | tf_op jit(solution)/shard_map/ppermute | solution.py:448
  14.6 3.7 %collective-permute-start.3 = (f32[2,16,2048]{2,1,0:T(8,128)}, f32[2,16,2048]{2,1,0:T(8,128)S(1)}, u32[]{:S(2)}, u32[]{:S(2)}) collective-permute-start(f32[2,16,2048]{2,1,0:T(8,128)} %get-tuple-element.7), channel_id=1, source_target_pairs={{1,2},{2,1},{3,4},{4,3},{5,6},{6,5},{7,8},{8,7},{9,10},{10,9},{11,... | collective-permute-start | bytes 786440 | tf_op jit(solution)/shard_map/ppermute | solution.py:449
  18.3 3.6 %all-to-all-done = f32[16,64,128]{2,1,0:T(8,128)S(1)} async-done(((f32[16,64,128]{2,1,0:T(8,128)}), f32[16,64,128]{2,1,0:T(8,128)S(1)}, u32[]{:S(2)}, u32[]{:S(2)}) %all-to-all-start) | async-done | bytes 524320 | tf_op jit(solution)/shard_map/all_to_all | solution.py:446
  21.9 7.4 %collective-permute-start = (f32[1024,128]{1,0:T(8,128)S(1)}, f32[1024,128]{1,0:T(8,128)S(1)}, u32[]{:S(2)}, u32[]{:S(2)}) collective-permute-start(f32[1024,128]{1,0:T(8,128)S(1)} %bitcast.41), channel_id=1, source_target_pairs={{0,16},{16,0},{32,48},{48,32},{64,80},{80,64},{96,112},{112,96},{1... | collective-permute-start | bytes 1572872 | tf_op jit(solution)/shard_map/ppermute | solution.py:453
  29.2 3.1 %collective-permute-start.1 = (f32[1024,128]{1,0:T(8,128)S(1)}, f32[1024,128]{1,0:T(8,128)S(1)}, u32[]{:S(2)}, u32[]{:S(2)}) collective-permute-start(f32[1024,128]{1,0:T(8,128)S(1)} %bitcast.42), channel_id=1, source_target_pairs={{16,32},{32,16},{48,64},{64,48},{80,96},{96,80},{17,33},{33,17},{4... | collective-permute-start | bytes 1572872 | tf_op jit(solution)/shard_map/ppermute | solution.py:454
  32.3 0.7 %multiply_bitcast_fusion.type_ref = s32[4096]{0:T(1024)S(1)} fusion(s32[128,32]{0,1:T(8,128)} %param.22), kind=kLoop, calls=%fused_computation.11 | loop fusion | flops 4096 | bytes 32768 | tf_op jit(solution)/shard_map/reshape | solution.py:459
  33.1 0.7 %fusion.2.src_ref = s32[4096]{0:T(1024)S(1)} fusion(s32[128,32]{0,1:T(8,128)} %param.21, s32[]{:T(128)S(6)} %xor.3, s32[]{:T(128)S(6)} %axis_index.27), kind=kLoop, calls=%fused_computation.7 | loop fusion | flops 102400 | bytes 32776 | tf_op jit(solution)/shard_map/reshape | solution.py:458
  33.8 0.7 %multiply_bitcast_fusion.1 = (s32[16,48]{1,0:T(8,128)S(1)}, s32[16,48]{1,0:T(8,128)S(1)}) fusion(s32[48,16]{0,1:T(8,128)} %param.19, s32[48,16]{0,1:T(8,128)} %param.18, s32[]{:T(128)S(6)} %sub.17), kind=kLoop, calls=%fused_computation.13 | loop fusion | flops 2304 | bytes 12292 | tf_op jit(solution)/shard_map/mul | solution.py:466
  34.5 0.0 collective-permute-done.2.pair_a_hbm
  34.5 0.0 collective-permute-done.3.pair_b_hbm
  34.5 6.9 %leaf_translate.1 = f32[2,48,2048]{2,1,0:T(8,128)} custom-call(s32[16,48]{1,0:T(8,128)S(1)} %get-tuple-element.9.src_hbm, s32[16,48]{1,0:T(8,128)S(1)} %get-tuple-element.8.type_hbm, f32[2,48,2048]{2,1,0:T(8,128)} %own_hbm.1, f32[2,16,2048]{2,1,0:T(8,128)S(1)} %collective-permute-done.2.pair_a_hbm, f32[2,16,2048]{2,1,0:T(8,128)S(1)} %collective-permute-done.3.pair_b_hbm, ...), custom_call_target="tpu_custom_call" | custom-call | flops 1000 | bytes 15000000 | tf_op jit(solution)/shard_map/leaf_translate/pallas_call | solution.py:397
  41.4 0.0 collective-permute-done.mate_hbm
  41.4 0.0 collective-permute-done.1.cross_hbm
  41.4 0.0 copy-done
  41.4 8.1 %top_translate.1 = f32[2,128,512]{2,1,0:T(8,128)} custom-call(s32[4096]{0:T(1024)S(1)} %fusion.2.src_ref, s32[4096]{0:T(1024)S(1)} %multiply_bitcast_fusion.type_ref, f32[1024,128]{1,0:T(8,128)S(1)} %bitcast.43, f32[1024,128]{1,0:T(8,128)S(1)} %collective-permute-done.mate_hbm, f32[1024,128]{1,0:T(8,128)S(1)} %collective-permute-done.1.cross_hbm, ...), custom_call_target="tpu_custom_call" | custom-call | flops 1000 | bytes 27000000 | tf_op jit(solution)/shard_map/top_translate/pallas_call | solution.py:274
Async XLA Ops:
  0.6 40.8 %copy-start = (f32[2,316,512]{2,0,1:T(2,128)S(1)}, f32[2,316,512]{2,0,1:T(2,128)}, u32[]{:S(2)}) copy-start(f32[2,316,512]{2,0,1:T(2,128)} %param.23) | copy-start | bytes 3883012
  5.6 16.2 %all-to-all-start = ((f32[16,64,128]{2,1,0:T(8,128)}), f32[16,64,128]{2,1,0:T(8,128)S(1)}, u32[]{:S(2)}, u32[]{:S(2)}) async-start(f32[16,64,128]{2,1,0:T(8,128)} %get-tuple-element.5), calls=%async_computation | async-start | bytes 1048576 | tf_op jit(solution)/shard_map/all_to_all | solution.py:446
  13.4 21.1 %collective-permute-start.2 = (f32[2,16,2048]{2,1,0:T(8,128)}, f32[2,16,2048]{2,1,0:T(8,128)S(1)}, u32[]{:S(2)}, u32[]{:S(2)}) collective-permute-start(f32[2,16,2048]{2,1,0:T(8,128)} %get-tuple-element.6), channel_id=1, source_target_pairs={{0,1},{1,0},{2,3},{3,2},{4,5},{5,4},{6,7},{7,6},{8,9},{9,8},{10,11... | collective-permute-start | bytes 786440 | tf_op jit(solution)/shard_map/ppermute | solution.py:448
  14.6 19.9 %collective-permute-start.3 = (f32[2,16,2048]{2,1,0:T(8,128)}, f32[2,16,2048]{2,1,0:T(8,128)S(1)}, u32[]{:S(2)}, u32[]{:S(2)}) collective-permute-start(f32[2,16,2048]{2,1,0:T(8,128)} %get-tuple-element.7), channel_id=1, source_target_pairs={{1,2},{2,1},{3,4},{4,3},{5,6},{6,5},{7,8},{8,7},{9,10},{10,9},{11,... | collective-permute-start | bytes 786440 | tf_op jit(solution)/shard_map/ppermute | solution.py:449
  21.9 19.5 %collective-permute-start = (f32[1024,128]{1,0:T(8,128)S(1)}, f32[1024,128]{1,0:T(8,128)S(1)}, u32[]{:S(2)}, u32[]{:S(2)}) collective-permute-start(f32[1024,128]{1,0:T(8,128)S(1)} %bitcast.41), channel_id=1, source_target_pairs={{0,16},{16,0},{32,48},{48,32},{64,80},{80,64},{96,112},{112,96},{1... | collective-permute-start | bytes 1572872 | tf_op jit(solution)/shard_map/ppermute | solution.py:453
  29.2 12.2 %collective-permute-start.1 = (f32[1024,128]{1,0:T(8,128)S(1)}, f32[1024,128]{1,0:T(8,128)S(1)}, u32[]{:S(2)}, u32[]{:S(2)}) collective-permute-start(f32[1024,128]{1,0:T(8,128)S(1)} %bitcast.42), channel_id=1, source_target_pairs={{16,32},{32,16},{48,64},{64,48},{80,96},{96,80},{17,33},{33,17},{4... | collective-permute-start | bytes 1572872 | tf_op jit(solution)/shard_map/ppermute | solution.py:454
